TPU v7x, 128 devices: a whole 4x4x4 slice. The times are simulated.
128 devices in a mesh: gx: 4 (over z_hi, core), gy: 8 (over z_lo, y), gz: 4 (over x).
Axes of the slice: x: 4, y: 4, z: 4 (z_hi: 2, z_lo: 2; z = z_hi * 2 + z_lo), core: 2. Of those that a mesh axis runs over, the one named last changes fastest.
Arguments:
- tokens: bfloat16 [1024, 6144], P('gx', ('gy', 'gz')), may hold values from -6 to 6
- weight_in: bfloat16 [6144, 24576], P('gy', ('gx', 'gz')), may hold values from -0.078125 to 0.078125
- weight_out: bfloat16 [24576, 6144], P(('gx', 'gz'), 'gy'), may hold values from -0.0390625 to 0.0390625
- grad_out: bfloat16 [1024, 6144], P('gx', ('gy', 'gz')), may hold values from -6 to 6
Outputs:
- out: bfloat16 [1024, 6144], P('gx', ('gy', 'gz'))
- grad_tokens: bfloat16 [1024, 6144], P('gx', ('gy', 'gz'))
- grad_weight_in: bfloat16 [6144, 24576], P('gy', ('gx', 'gz'))
- grad_weight_out: bfloat16 [24576, 6144], P(('gx', 'gz'), 'gy')
All inputs are finite; a program needn't handle non-finite values.
Results may differ from a plain program's by a relative error of at most 0.025.
Values may be sent and summed in bfloat16 or wider, within the bound.
No kernel may reach another device: no remote copies, remote signals or barrier semaphores. Data moves between devices by JAX's collectives and lax.ppermute only.
A program may use at most 128 MiB of HBM per device.

v0:
```python
import jax
import jax.numpy as jnp
from jax import lax
from jax.experimental import pallas as pl
from jax.experimental.pallas import tpu as pltpu
from jax.sharding import PartitionSpec as P

half_root = 0.7071067811865476
inv_root_tau = 0.3989422804014327
bf16 = jnp.bfloat16
f32 = jnp.float32


def gelu_value(preact):
    return 0.5 * preact * (1.0 + jax.scipy.special.erf(preact * half_root))


def gelu_slope(preact):
    return 0.5 * (
        1.0 + jax.scipy.special.erf(preact * half_root)
    ) + preact * inv_root_tau * jnp.exp(-0.5 * preact * preact)


def dot_nn(left, right):
    return lax.dot_general(left, right, (((1,), (0,)), ((), ())), preferred_element_type=f32)


def dot_tn(left, right):
    return lax.dot_general(left, right, (((0,), (0,)), ((), ())), preferred_element_type=f32)


def dot_nt(left, right):
    return lax.dot_general(left, right, (((1,), (1,)), ((), ())), preferred_element_type=f32)


def corner(place):
    return place ^ (place >> 1)


GY_PAIRS = {
    2: [(g, g ^ 4) for g in range(8)],
    1: [(g, (g & 4) | (3 - (g & 3))) for g in range(8)],
    0: [(g, g ^ 1) for g in range(8)],
}
GZ_PAIRS = {step: [(g, corner(corner(g) ^ step)) for g in range(4)] for step in (1, 2, 3)}
CORE_PAIRS = [(g, g ^ 1) for g in range(4)]
HIGH_PAIRS = [(g, g ^ 2) for g in range(4)]

PARTS = 3
ORDERS = ((2, 1, 0), (1, 0, 2), (0, 2, 1))
SLOT = 256


def over_gy(block, bit):
    return lax.ppermute(block, "gy", GY_PAIRS[bit])


def over_gz(block, step):
    return lax.ppermute(block, "gz", GZ_PAIRS[step])


def over_core(block):
    return lax.ppermute(block, "gx", CORE_PAIRS)


def over_high(block):
    return lax.ppermute(block, "gx", HIGH_PAIRS)


def pick(array, axis, index):
    return lax.index_in_dim(array, index, axis, keepdims=False)


def dyn(array, index):
    return lax.dynamic_index_in_dim(array, index, 0, keepdims=False)


def pass_on(*refs):
    pass


def gate(values, last):
    values, last = tuple(values), tuple(last)
    anywhere = pl.BlockSpec(memory_space=pl.ANY)
    return pl.pallas_call(
        pass_on,
        out_shape=[jax.ShapeDtypeStruct(v.shape, v.dtype) for v in values],
        in_specs=[anywhere] * (len(values) + len(last)),
        out_specs=[anywhere] * len(values),
        input_output_aliases={i: i for i in range(len(values))},
        compiler_params=pltpu.CompilerParams(vmem_limit_bytes=1 << 20),
    )(*values, *last)


def per_device(tokens, weight_in, weight_out, grad_out):
    gy = lax.axis_index("gy")
    gy_id = (gy & 4) | corner(gy & 3)
    gz_id = corner(lax.axis_index("gz"))
    rows = tokens.shape[0] // 8
    width = tokens.shape[1]
    hidden = weight_in.shape[1]
    part = hidden // PARTS
    slot = max(SLOT, width)
    depth = 4 * width

    both = jnp.concatenate([tokens, grad_out], axis=1).reshape(8, rows, 2 * width)
    own = jnp.stack([dyn(both, p ^ gy_id) for p in range(8)])
    squares = [jnp.stack([half] + [over_gz(half, step) for step in (1, 2, 3)]) for half in (own, over_high(own))]
    squares = [[dyn(square, corner(p) ^ gz_id) for p in range(4)] for square in squares]
    sides = []
    for lo in (0, width):
        spread = [jnp.concatenate([s[..., lo : lo + width] for s in square], axis=-1) for square in squares]
        mine = jnp.stack(spread, axis=1)
        sides.append(jnp.stack([mine, over_core(mine)], axis=1).reshape(2, 2, 2, 2, 2, rows, depth))
    features, grad_feats = sides

    def add(left, right):
        return left.astype(f32) + right.astype(f32)

    spans = [(i * part, (i + 1) * part) for i in range(PARTS)]
    terms = dot_nn(features.reshape(-1, depth), weight_in).astype(bf16).reshape(2, 2, 2, 4 * rows, hidden)
    grad_terms = dot_nt(grad_feats.reshape(-1, depth), weight_out).astype(bf16).reshape(2, 2, 2, 4 * rows, hidden)
    cubes = ([], [])
    for (lo, hi), (first, second, third) in zip(spans, ORDERS):
        axis = 1 + [bit for bit in (2, 1, 0) if bit != first].index(second)
        away, held = (
            jnp.stack([pick(side[..., lo:hi], 2 - first, k) for side in (terms, grad_terms)]) for k in (1, 0)
        )
        held = add(held, over_gy(away, first)).astype(bf16)
        held = add(pick(held, axis, 0), over_gy(pick(held, axis, 1), second)).astype(bf16)
        if not cubes[0]:
            begun = held
        total = add(held[:, 0], over_gy(held[:, 1], third))
        active = gelu_value(total[0]).astype(bf16)
        grad = (total[1] * gelu_slope(total[0])).astype(bf16)
        piece = jnp.stack([active, grad])
        pair = jnp.stack([piece, over_gy(piece, third)], axis=1)
        square = jnp.stack([pair, over_gy(pair, second)], axis=1)
        axes = [(first, second, third).index(bit) for bit in (2, 1, 0)]
        for side, full in zip(square, cubes):
            cube = jnp.stack([side, over_gy(side, first)])
            full.append(cube.transpose(*axes, 3, 4).reshape(2, 2, 2, 2, 2, rows, part))
    active_rows, grad_rows = (jnp.concatenate(full, axis=-1) for full in cubes)

    gz_late = gz_id + (begun[0, 0, 0, 0].astype(f32) * 0.0).astype(jnp.int32)

    def slots(pieces, axis, fill):
        full = []
        for p in range(4):
            place = corner(p ^ gz_late)
            low = jnp.where(place & 1 == 1, pieces[1], pieces[0])
            high = jnp.where(place & 1 == 1, pieces[3], pieces[2])
            piece = jnp.where(place >= 2, high, low)
            wide = [(0, 0), (0, 0)]
            wide[axis] = fill
            full.append(jnp.pad(piece, wide))
        return jnp.concatenate(full, axis=axis)

    slots_out = slots([weight_out[:, p * width : (p + 1) * width] for p in range(4)], 1, (0, slot - width))
    slots_in = slots([weight_in[p * width : (p + 1) * width] for p in range(4)], 0, (slot - width, 0))

    def core_sum(times, full):
        away = times(full[:, :, :, 1].reshape(-1, hidden)).astype(bf16)
        return add(times(full[:, :, :, 0].reshape(-1, hidden)), over_core(away)).astype(bf16)

    out_mine = core_sum(lambda u: dot_nn(u, slots_out), active_rows)
    grad_mine = core_sum(lambda u: dot_nt(u, slots_in), grad_rows)
    lap = slot // 2

    def joined(p):
        left, right = (side[:, p * slot : (p + 1) * slot] for side in (out_mine, grad_mine))
        return jnp.concatenate([left[:, :lap], left[:, lap:] + right[:, :lap], right[:, lap:]], axis=1)

    got = [over_gz(joined(step), step) for step in (1, 2, 3)]
    features, grad_feats = gate([features, grad_feats], [out_mine, grad_mine])
    grad_weight_out = dot_tn(active_rows.reshape(-1, hidden), grad_feats.reshape(-1, depth)).astype(bf16)
    grad_weight_in = dot_tn(features.reshape(-1, depth), grad_rows.reshape(-1, hidden)).astype(bf16)
    total = joined(0).astype(f32)
    for block in gate(got, [grad_weight_out, grad_weight_in]):
        total += block.astype(f32)
    total = total.reshape(8, 2, rows, 3 * lap)
    total = add(total[:, 0], over_high(total[:, 1].astype(bf16))).astype(bf16)
    total = jnp.concatenate([dyn(total, p ^ gy_id) for p in range(8)], axis=0)
    return (total[:, :width], total[:, -width:], grad_weight_in, grad_weight_out)


def solution(mesh):
    return jax.shard_map(
        per_device,
        mesh=mesh,
        in_specs=(
            P("gx", ("gy", "gz")),
            P("gy", ("gx", "gz")),
            P(("gx", "gz"), "gy"),
            P("gx", ("gy", "gz")),
        ),
        out_specs=(
            P("gx", ("gy", "gz")),
            P("gx", ("gy", "gz")),
            P("gy", ("gx", "gz")),
            P(("gx", "gz"), "gy"),
        ),
        check_vma=False,
    )
```

profile of v0, /device:TPU:0, one launch (start us, length us, event | category | flops | bytes accessed | tf_op | source)
XLA Modules:
  0.0 186.5 jit_solution(11213128576922082889)
XLA Ops:
  3.0 4.0 %collective-permute-start.3 = (bf16[8,32,384]{2,1,0:T(8,128)(2,1)S(1)}, bf16[8,32,384]{2,1,0:T(8,128)(2,1)S(1)}, u32[]{:S(2)}, u32[]{:S(2)}) collective-permute-start(bf16[8,32,384]{2,1,0:T(8,128)(2,1)S(1)} %dynamic-slice_dynamic-update-slice_fusion), channel_id=1, source_target_pairs={{0,64},{32,96},{64,0},{96,32},{1,65},{33,97},{65,1},{97,33},{2,66}... | collective-permute-start | bytes 589832 | tf_op jit(solution)/shard_map/ppermute | solution.py:67
  7.0 3.0 %collective-permute-start.2 = (bf16[8,32,384]{2,1,0:T(8,128)(2,1)S(1)}, bf16[8,32,384]{2,1,0:T(8,128)(2,1)S(1)}, u32[]{:S(2)}, u32[]{:S(2)}) collective-permute-start(bf16[8,32,384]{2,1,0:T(8,128)(2,1)S(1)} %dynamic-slice_dynamic-update-slice_fusion), channel_id=1, source_target_pairs={{0,2},{1,3},{2,0},{3,1},{4,6},{5,7},{6,4},{7,5},{8,10},{9,11},{10,... | collective-permute-start | bytes 589832 | tf_op jit(solution)/shard_map/ppermute | solution.py:59
  11.9 3.0 %collective-permute-start.6 = (bf16[8,32,384]{2,1,0:T(8,128)(2,1)S(1)}, bf16[8,32,384]{2,1,0:T(8,128)(2,1)S(1)}, u32[]{:S(2)}, u32[]{:S(2)}) collective-permute-start(bf16[8,32,384]{2,1,0:T(8,128)(2,1)S(1)} %collective-permute-done.3), channel_id=1, source_target_pairs={{0,2},{1,3},{2,0},{3,1},{4,6},{5,7},{6,4},{7,5},{8,10},{9,11},{10,... | collective-permute-start | bytes 589832 | tf_op jit(solution)/shard_map/ppermute | solution.py:59
  17.9 4.4 %collective-permute-done.1 = bf16[8,32,384]{2,1,0:T(8,128)(2,1)S(1)} collective-permute-done((bf16[8,32,384]{2,1,0:T(8,128)(2,1)S(1)}, bf16[8,32,384]{2,1,0:T(8,128)(2,1)S(1)}, u32[]{:S(2)}, u32[]{:S(2)}) %collective-permute-start.1) | collective-permute-done | bytes 196640 | tf_op jit(solution)/shard_map/ppermute | solution.py:59
  22.4 2.4 %collective-permute-done.6 = bf16[8,32,384]{2,1,0:T(8,128)(2,1)S(1)} collective-permute-done((bf16[8,32,384]{2,1,0:T(8,128)(2,1)S(1)}, bf16[8,32,384]{2,1,0:T(8,128)(2,1)S(1)}, u32[]{:S(2)}, u32[]{:S(2)}) %collective-permute-start.6) | collective-permute-done | bytes 196640 | tf_op jit(solution)/shard_map/ppermute | solution.py:59
  24.8 2.7 %collective-permute-done.5 = bf16[8,32,384]{2,1,0:T(8,128)(2,1)S(1)} collective-permute-done((bf16[8,32,384]{2,1,0:T(8,128)(2,1)S(1)}, bf16[8,32,384]{2,1,0:T(8,128)(2,1)S(1)}, u32[]{:S(2)}, u32[]{:S(2)}) %collective-permute-start.5) | collective-permute-done | bytes 196640 | tf_op jit(solution)/shard_map/ppermute | solution.py:59
  34.8 2.9 %convolution_convert_fusion = bf16[1024,1536]{1,0:T(8,128)(2,1)S(1)} fusion(bf16[1024,768]{1,0:T(8,128)(2,1)S(1)} %bitcast.261, bf16[1536,768]{1,0:T(8,128)(2,1)S(1)} %copy-done.2), kind=kOutput, calls=%fused_computation.26 | convolution fusion | flops 2417491968 | bytes 7077888 | tf_op jit(solution)/shard_map/dot_general | solution.py:33
  39.8 2.8 %convolution_convert_fusion.1 = bf16[1024,1536]{1,0:T(8,128)(2,1)S(1)} fusion(bf16[1024,768]{1,0:T(8,128)(2,1)S(1)} %bitcast.262, bf16[768,1536]{1,0:T(8,128)(2,1)S(1)} %copy-done.3), kind=kOutput, calls=%fused_computation.27 | convolution fusion | flops 2417491968 | bytes 7077888 | tf_op jit(solution)/shard_map/dot_general | solution.py:25
  46.1 2.3 %collective-permute-start.15 = (bf16[2,2,2,128,512]{4,3,0,1,2:T(8,128)(2,1)S(1)}, bf16[2,2,2,128,512]{4,3,0,1,2:T(8,128)(2,1)S(1)}, u32[]{:S(2)}, u32[]{:S(2)}) collective-permute-start(bf16[2,2,2,128,512]{4,3,0,1,2:T(8,128)(2,1)S(1)} %pad_maximum_fusion.7), channel_id=1, source_target_pairs={{0,12},{4,8},{8,4},{12,0},{16,28},{20,24},{24,20},{28,16},{1,13},{... | collective-permute-start | bytes 3145736 | tf_op jit(solution)/shard_map/ppermute | solution.py:55
  48.5 19.5 %collective-permute-done.21 = bf16[2,2,2,128,512]{4,3,2,1,0:T(8,128)(2,1)S(1)} collective-permute-done((bf16[2,2,2,128,512]{4,3,2,1,0:T(8,128)(2,1)S(1)}, bf16[2,2,2,128,512]{4,3,2,1,0:T(8,128)(2,1)S(1)}, u32[]{:S(2)}, u32[]{:S(2)}) %collective-permute-start.21) | collective-permute-done | bytes 1048608 | tf_op jit(solution)/shard_map/ppermute | solution.py:55
  69.9 2.9 %collective-permute-start.10 = (bf16[2,2,128,512]{3,2,0,1:T(8,128)(2,1)S(1)}, bf16[2,2,128,512]{3,2,0,1:T(8,128)(2,1)S(1)}, u32[]{:S(2)}, u32[]{:S(2)}) collective-permute-start(bf16[2,2,128,512]{3,2,0,1:T(8,128)(2,1)S(1)} %slice_bitcast_fusion.8), channel_id=1, source_target_pairs={{0,12},{4,8},{8,4},{12,0},{16,28},{20,24},{24,20},{28,16},{1,13},{... | collective-permute-start | bytes 1572872 | tf_op jit(solution)/shard_map/ppermute | solution.py:55
  74.1 7.2 %collective-permute-done.22 = bf16[2,2,128,512]{3,2,1,0:T(8,128)(2,1)S(1)} collective-permute-done((bf16[2,2,128,512]{3,2,1,0:T(8,128)(2,1)S(1)}, bf16[2,2,128,512]{3,2,1,0:T(8,128)(2,1)S(1)}, u32[]{:S(2)}, u32[]{:S(2)}) %collective-permute-start.22) | collective-permute-done | bytes 524320 | tf_op jit(solution)/shard_map/ppermute | solution.py:55
  87.7 2.9 %collective-permute-start.23 = (bf16[2,128,512]{2,1,0:T(8,128)(2,1)}, bf16[2,128,512]{2,1,0:T(8,128)(2,1)}, u32[]{:S(2)}, u32[]{:S(2)}) collective-permute-start(bf16[2,128,512]{2,1,0:T(8,128)(2,1)} %slice_bitcast_fusion.15), channel_id=1, source_target_pairs={{0,12},{4,8},{8,4},{12,0},{16,28},{20,24},{24,20},{28,16},{1,13},{... | collective-permute-start | bytes 786440 | tf_op jit(solution)/shard_map/ppermute | solution.py:55
  103.1 3.4 %collective-permute-done.24 = bf16[2,128,512]{2,1,0:T(8,128)(2,1)S(1)} collective-permute-done((bf16[2,128,512]{2,1,0:T(8,128)(2,1)S(1)}, bf16[2,128,512]{2,1,0:T(8,128)(2,1)S(1)}, u32[]{:S(2)}, u32[]{:S(2)}) %collective-permute-start.24) | collective-permute-done | bytes 262176 | tf_op jit(solution)/shard_map/ppermute | solution.py:55
  107.7 2.7 %collective-permute-done.18 = bf16[2,128,512]{2,1,0:T(8,128)(2,1)S(1)} collective-permute-done((bf16[2,128,512]{2,1,0:T(8,128)(2,1)S(1)}, bf16[2,128,512]{2,1,0:T(8,128)(2,1)S(1)}, u32[]{:S(2)}, u32[]{:S(2)}) %collective-permute-start.18) | collective-permute-done | bytes 262176 | tf_op jit(solution)/shard_map/ppermute | solution.py:55
  113.4 5.7 %collective-permute-done.25 = bf16[2,2,128,512]{3,2,0,1:T(8,128)(2,1)S(1)} collective-permute-done((bf16[2,2,128,512]{3,2,0,1:T(8,128)(2,1)S(1)}, bf16[2,2,128,512]{3,2,0,1:T(8,128)(2,1)S(1)}, u32[]{:S(2)}, u32[]{:S(2)}) %collective-permute-start.25) | collective-permute-done | bytes 524320 | tf_op jit(solution)/shard_map/ppermute | solution.py:55
  119.3 1.9 %collective-permute-done.19 = bf16[2,2,128,512]{3,2,0,1:T(8,128)(2,1)S(1)} collective-permute-done((bf16[2,2,128,512]{3,2,0,1:T(8,128)(2,1)S(1)}, bf16[2,2,128,512]{3,2,0,1:T(8,128)(2,1)S(1)}, u32[]{:S(2)}, u32[]{:S(2)}) %collective-permute-start.19) | collective-permute-done | bytes 524320 | tf_op jit(solution)/shard_map/ppermute | solution.py:55
  121.3 2.0 %collective-permute-start.20 = (bf16[2,2,128,512]{3,2,1,0:T(8,128)(2,1)S(1)}, bf16[2,2,128,512]{3,2,1,0:T(8,128)(2,1)S(1)}, u32[]{:S(2)}, u32[]{:S(2)}) collective-permute-start(bf16[2,2,128,512]{3,2,1,0:T(8,128)(2,1)S(1)} %bitcast.256), channel_id=1, source_target_pairs={{0,12},{4,8},{8,4},{12,0},{16,28},{20,24},{24,20},{28,16},{1,13},{... | collective-permute-start | bytes 1572872 | tf_op jit(solution)/shard_map/ppermute | solution.py:55
  127.3 10.2 %collective-permute-done.20 = bf16[2,2,128,512]{3,2,1,0:T(8,128)(2,1)S(1)} collective-permute-done((bf16[2,2,128,512]{3,2,1,0:T(8,128)(2,1)S(1)}, bf16[2,2,128,512]{3,2,1,0:T(8,128)(2,1)S(1)}, u32[]{:S(2)}, u32[]{:S(2)}) %collective-permute-start.20) | collective-permute-done | bytes 524320 | tf_op jit(solution)/shard_map/ppermute | solution.py:55
  141.4 3.6 %collective-permute-done.29 = bf16[2,2,128,512]{3,2,1,0:T(8,128)(2,1)S(1)} collective-permute-done((bf16[2,2,128,512]{3,2,1,0:T(8,128)(2,1)S(1)}, bf16[2,2,128,512]{3,2,1,0:T(8,128)(2,1)S(1)}, u32[]{:S(2)}, u32[]{:S(2)}) %collective-permute-start.29) | collective-permute-done | bytes 524320 | tf_op jit(solution)/shard_map/ppermute | solution.py:55
  159.4 3.5 %bitcast_convert_fusion.1.refs_3_ = bf16[1536,768]{1,0:T(8,128)(2,1)S(1)} fusion(bf16[2,2,2,2,2,32,768]{6,5,4,3,2,1,0:T(8,128)(2,1)S(1)} %get-tuple-element.9, bf16[2,2,2,2,2,32,512]{6,5,4,3,2,1,0:T(8,128)(2,1)S(1)} %bitcast.226, bf16[2,2,2,2,2,32,512]{6,5,4,3,2,1,0:T(8,128)(2,1)S(1)} %bitcast.224, bf16[1,2,2,2,2,32,512]{6,5,4,3,2,1,0:T(8,128)(2,1)S(1)} %bitcast.276, ...), kind=kOutput, calls=%fused_computation.25 | convolution fusion | flops 2429681664 | bytes 7077888 | tf_op jit(solution)/shard_map/dot_general | solution.py:29
  162.9 3.2 %bitcast_convert_fusion.refs_4_ = bf16[768,1536]{1,0:T(8,128)(2,1)S(1)} fusion(bf16[2,2,2,2,2,32,768]{6,5,4,3,2,1,0:T(8,128)(2,1)S(1)} %get-tuple-element.10, bf16[2,2,2,2,2,32,512]{6,5,4,3,2,1,0:T(8,128)(2,1)S(1)} %bitcast.230, bf16[2,2,2,2,2,32,512]{6,5,4,3,2,1,0:T(8,128)(2,1)S(1)} %bitcast.228, bf16[1,2,2,2,2,32,512]{6,5,4,3,2,1,0:T(8,128)(2,1)S(1)} %bitcast.278, ...), kind=kOutput, calls=%fused_computation.24 | convolution fusion | flops 2429681664 | bytes 7077888 | tf_op jit(solution)/shard_map/dot_general | solution.py:29
  167.0 9.9 %collective-permute-done.33.refs_1_ = bf16[512,384]{1,0:T(8,128)(2,1)S(1)} collective-permute-done((bf16[512,384]{1,0:T(8,128)(2,1)S(1)}, bf16[512,384]{1,0:T(8,128)(2,1)S(1)}, u32[]{:S(2)}, u32[]{:S(2)}) %collective-permute-start.33) | collective-permute-done | bytes 393248 | tf_op jit(solution)/shard_map/ppermute | solution.py:59
  178.4 6.0 %collective-permute-done.35 = bf16[8,32,384]{2,1,0:T(8,128)(2,1)S(1)} collective-permute-done((bf16[8,32,384]{2,1,0:T(8,128)(2,1)S(1)}, bf16[8,32,384]{2,1,0:T(8,128)(2,1)S(1)}, u32[]{:S(2)}, u32[]{:S(2)}) %collective-permute-start.35) | collective-permute-done | bytes 196640 | tf_op jit(solution)/shard_map/ppermute | solution.py:67
  (231 shorter events, 71.8 us)
Async XLA Ops:
  10.0 12.2 %collective-permute-start.1 = (bf16[8,32,384]{2,1,0:T(8,128)(2,1)S(1)}, bf16[8,32,384]{2,1,0:T(8,128)(2,1)S(1)}, u32[]{:S(2)}, u32[]{:S(2)}) collective-permute-start(bf16[8,32,384]{2,1,0:T(8,128)(2,1)S(1)} %dynamic-slice_dynamic-update-slice_fusion), channel_id=1, source_target_pairs={{0,3},{1,2},{2,1},{3,0},{4,7},{5,6},{6,5},{7,4},{8,11},{9,10},{10,... | collective-permute-start | bytes 589832 | tf_op jit(solution)/shard_map/ppermute | solution.py:59
  11.2 11.1 %collective-permute-start = (bf16[8,32,384]{2,1,0:T(8,128)(2,1)S(1)}, bf16[8,32,384]{2,1,0:T(8,128)(2,1)S(1)}, u32[]{:S(2)}, u32[]{:S(2)}) collective-permute-start(bf16[8,32,384]{2,1,0:T(8,128)(2,1)S(1)} %dynamic-slice_dynamic-update-slice_fusion), channel_id=1, source_target_pairs={{0,1},{1,0},{2,3},{3,2},{4,5},{5,4},{6,7},{7,6},{8,9},{9,8},{10,11... | collective-permute-start | bytes 589832 | tf_op jit(solution)/shard_map/ppermute | solution.py:59
  11.9 12.9 %collective-permute-start.6 = (bf16[8,32,384]{2,1,0:T(8,128)(2,1)S(1)}, bf16[8,32,384]{2,1,0:T(8,128)(2,1)S(1)}, u32[]{:S(2)}, u32[]{:S(2)}) collective-permute-start(bf16[8,32,384]{2,1,0:T(8,128)(2,1)S(1)} %collective-permute-done.3), channel_id=1, source_target_pairs={{0,2},{1,3},{2,0},{3,1},{4,6},{5,7},{6,4},{7,5},{8,10},{9,11},{10,... | collective-permute-start | bytes 589832 | tf_op jit(solution)/shard_map/ppermute | solution.py:59
  14.9 12.6 %collective-permute-start.5 = (bf16[8,32,384]{2,1,0:T(8,128)(2,1)S(1)}, bf16[8,32,384]{2,1,0:T(8,128)(2,1)S(1)}, u32[]{:S(2)}, u32[]{:S(2)}) collective-permute-start(bf16[8,32,384]{2,1,0:T(8,128)(2,1)S(1)} %collective-permute-done.3), channel_id=1, source_target_pairs={{0,3},{1,2},{2,1},{3,0},{4,7},{5,6},{6,5},{7,4},{8,11},{9,10},{10,... | collective-permute-start | bytes 589832 | tf_op jit(solution)/shard_map/ppermute | solution.py:59
  16.1 11.6 %collective-permute-start.4 = (bf16[8,32,384]{2,1,0:T(8,128)(2,1)S(1)}, bf16[8,32,384]{2,1,0:T(8,128)(2,1)S(1)}, u32[]{:S(2)}, u32[]{:S(2)}) collective-permute-start(bf16[8,32,384]{2,1,0:T(8,128)(2,1)S(1)} %collective-permute-done.3), channel_id=1, source_target_pairs={{0,1},{1,0},{2,3},{3,2},{4,5},{5,4},{6,7},{7,6},{8,9},{9,8},{10,11... | collective-permute-start | bytes 589832 | tf_op jit(solution)/shard_map/ppermute | solution.py:59
  42.8 25.2 %collective-permute-start.21 = (bf16[2,2,2,128,512]{4,3,2,1,0:T(8,128)(2,1)S(1)}, bf16[2,2,2,128,512]{4,3,2,1,0:T(8,128)(2,1)S(1)}, u32[]{:S(2)}, u32[]{:S(2)}) collective-permute-start(bf16[2,2,2,128,512]{4,3,2,1,0:T(8,128)(2,1)S(1)} %pad_maximum_fusion.8), channel_id=1, source_target_pairs={{0,4},{4,0},{8,12},{12,8},{16,20},{20,16},{24,28},{28,24},{1,5},{5... | collective-permute-start | bytes 3145736 | tf_op jit(solution)/shard_map/ppermute | solution.py:55
  44.6 24.9 %collective-permute-start.9 = (bf16[2,2,2,128,512]{4,3,0,2,1:T(8,128)(2,1)S(1)}, bf16[2,2,2,128,512]{4,3,0,2,1:T(8,128)(2,1)S(1)}, u32[]{:S(2)}, u32[]{:S(2)}) collective-permute-start(bf16[2,2,2,128,512]{4,3,0,2,1:T(8,128)(2,1)S(1)} %pad_maximum_fusion.6), channel_id=1, source_target_pairs={{0,16},{4,20},{8,24},{12,28},{16,0},{20,4},{24,8},{28,12},{1,17},{... | collective-permute-start | bytes 3145736 | tf_op jit(solution)/shard_map/ppermute | solution.py:55
  46.1 26.7 %collective-permute-start.15 = (bf16[2,2,2,128,512]{4,3,0,1,2:T(8,128)(2,1)S(1)}, bf16[2,2,2,128,512]{4,3,0,1,2:T(8,128)(2,1)S(1)}, u32[]{:S(2)}, u32[]{:S(2)}) collective-permute-start(bf16[2,2,2,128,512]{4,3,0,1,2:T(8,128)(2,1)S(1)} %pad_maximum_fusion.7), channel_id=1, source_target_pairs={{0,12},{4,8},{8,4},{12,0},{16,28},{20,24},{24,20},{28,16},{1,13},{... | collective-permute-start | bytes 3145736 | tf_op jit(solution)/shard_map/ppermute | solution.py:55
  68.3 13.1 %collective-permute-start.22 = (bf16[2,2,128,512]{3,2,1,0:T(8,128)(2,1)S(1)}, bf16[2,2,128,512]{3,2,1,0:T(8,128)(2,1)S(1)}, u32[]{:S(2)}, u32[]{:S(2)}) collective-permute-start(bf16[2,2,128,512]{3,2,1,0:T(8,128)(2,1)S(1)} %slice_bitcast_fusion), channel_id=1, source_target_pairs={{0,16},{4,20},{8,24},{12,28},{16,0},{20,4},{24,8},{28,12},{1,17},{... | collective-permute-start | bytes 1572872 | tf_op jit(solution)/shard_map/ppermute | solution.py:55
  69.9 14.0 %collective-permute-start.10 = (bf16[2,2,128,512]{3,2,0,1:T(8,128)(2,1)S(1)}, bf16[2,2,128,512]{3,2,0,1:T(8,128)(2,1)S(1)}, u32[]{:S(2)}, u32[]{:S(2)}) collective-permute-start(bf16[2,2,128,512]{3,2,0,1:T(8,128)(2,1)S(1)} %slice_bitcast_fusion.8), channel_id=1, source_target_pairs={{0,12},{4,8},{8,4},{12,0},{16,28},{20,24},{24,20},{28,16},{1,13},{... | collective-permute-start | bytes 1572872 | tf_op jit(solution)/shard_map/ppermute | solution.py:55
  74.0 18.2 %collective-permute-start.16 = (bf16[2,2,128,512]{3,2,0,1:T(8,128)(2,1)}, bf16[2,2,128,512]{3,2,0,1:T(8,128)(2,1)}, u32[]{:S(2)}, u32[]{:S(2)}) collective-permute-start(bf16[2,2,128,512]{3,2,0,1:T(8,128)(2,1)} %slice_bitcast_fusion.6), channel_id=1, source_target_pairs={{0,4},{4,0},{8,12},{12,8},{16,20},{20,16},{24,28},{28,24},{1,5},{5... | collective-permute-start | bytes 1572872 | tf_op jit(solution)/shard_map/ppermute | solution.py:55
  87.7 9.5 %collective-permute-start.23 = (bf16[2,128,512]{2,1,0:T(8,128)(2,1)}, bf16[2,128,512]{2,1,0:T(8,128)(2,1)}, u32[]{:S(2)}, u32[]{:S(2)}) collective-permute-start(bf16[2,128,512]{2,1,0:T(8,128)(2,1)} %slice_bitcast_fusion.15), channel_id=1, source_target_pairs={{0,12},{4,8},{8,4},{12,0},{16,28},{20,24},{24,20},{28,16},{1,13},{... | collective-permute-start | bytes 786440 | tf_op jit(solution)/shard_map/ppermute | solution.py:55
  106.6 12.5 %collective-permute-start.25 = (bf16[2,2,128,512]{3,2,0,1:T(8,128)(2,1)S(1)}, bf16[2,2,128,512]{3,2,0,1:T(8,128)(2,1)S(1)}, u32[]{:S(2)}, u32[]{:S(2)}) collective-permute-start(bf16[2,2,128,512]{3,2,0,1:T(8,128)(2,1)S(1)} %get-tuple-element.79), channel_id=1, source_target_pairs={{0,16},{4,20},{8,24},{12,28},{16,0},{20,4},{24,8},{28,12},{1,17},{... | collective-permute-start | bytes 1572872 | tf_op jit(solution)/shard_map/ppermute | solution.py:55
  110.4 10.8 %collective-permute-start.19 = (bf16[2,2,128,512]{3,2,0,1:T(8,128)(2,1)S(1)}, bf16[2,2,128,512]{3,2,0,1:T(8,128)(2,1)S(1)}, u32[]{:S(2)}, u32[]{:S(2)}) collective-permute-start(bf16[2,2,128,512]{3,2,0,1:T(8,128)(2,1)S(1)} %get-tuple-element.75), channel_id=1, source_target_pairs={{0,4},{4,0},{8,12},{12,8},{16,20},{20,16},{24,28},{28,24},{1,5},{5... | collective-permute-start | bytes 1572872 | tf_op jit(solution)/shard_map/ppermute | solution.py:55
  112.1 12.0 %collective-permute-start.13 = (bf16[2,2,128,512]{3,2,0,1:T(8,128)(2,1)S(1)}, bf16[2,2,128,512]{3,2,0,1:T(8,128)(2,1)S(1)}, u32[]{:S(2)}, u32[]{:S(2)}) collective-permute-start(bf16[2,2,128,512]{3,2,0,1:T(8,128)(2,1)S(1)} %get-tuple-element.71), channel_id=1, source_target_pairs={{0,12},{4,8},{8,4},{12,0},{16,28},{20,24},{24,20},{28,16},{1,13},{... | collective-permute-start | bytes 1572872 | tf_op jit(solution)/shard_map/ppermute | solution.py:55
  119.2 19.5 %collective-permute-start.26 = (bf16[2,2,128,512]{3,2,1,0:T(8,128)(2,1)S(1)}, bf16[2,2,128,512]{3,2,1,0:T(8,128)(2,1)S(1)}, u32[]{:S(2)}, u32[]{:S(2)}) collective-permute-start(bf16[2,2,128,512]{3,2,1,0:T(8,128)(2,1)S(1)} %bitcast.255), channel_id=1, source_target_pairs={{0,4},{4,0},{8,12},{12,8},{16,20},{20,16},{24,28},{28,24},{1,5},{5... | collective-permute-start | bytes 1572872 | tf_op jit(solution)/shard_map/ppermute | solution.py:55
  121.3 16.1 %collective-permute-start.20 = (bf16[2,2,128,512]{3,2,1,0:T(8,128)(2,1)S(1)}, bf16[2,2,128,512]{3,2,1,0:T(8,128)(2,1)S(1)}, u32[]{:S(2)}, u32[]{:S(2)}) collective-permute-start(bf16[2,2,128,512]{3,2,1,0:T(8,128)(2,1)S(1)} %bitcast.256), channel_id=1, source_target_pairs={{0,12},{4,8},{8,4},{12,0},{16,28},{20,24},{24,20},{28,16},{1,13},{... | collective-permute-start | bytes 1572872 | tf_op jit(solution)/shard_map/ppermute | solution.py:55
  124.2 14.6 %collective-permute-start.14 = (bf16[2,2,128,512]{3,2,1,0:T(8,128)(2,1)S(1)}, bf16[2,2,128,512]{3,2,1,0:T(8,128)(2,1)S(1)}, u32[]{:S(2)}, u32[]{:S(2)}) collective-permute-start(bf16[2,2,128,512]{3,2,1,0:T(8,128)(2,1)S(1)} %bitcast.246), channel_id=1, source_target_pairs={{0,16},{4,20},{8,24},{12,28},{16,0},{20,4},{24,8},{28,12},{1,17},{... | collective-permute-start | bytes 1572872 | tf_op jit(solution)/shard_map/ppermute | solution.py:55
  125.6 19.7 %collective-permute-start.30 = (bf16[2,2,128,512]{3,2,1,0:T(8,128)(2,1)S(1)}, bf16[2,2,128,512]{3,2,1,0:T(8,128)(2,1)S(1)}, u32[]{:S(2)}, u32[]{:S(2)}) collective-permute-start(bf16[2,2,128,512]{3,2,1,0:T(8,128)(2,1)S(1)} %bitcast.253), channel_id=1, source_target_pairs={{0,4},{4,0},{8,12},{12,8},{16,20},{20,16},{24,28},{28,24},{1,5},{5... | collective-permute-start | bytes 1572872 | tf_op jit(solution)/shard_map/ppermute | solution.py:55
  126.2 18.8 %collective-permute-start.29 = (bf16[2,2,128,512]{3,2,1,0:T(8,128)(2,1)S(1)}, bf16[2,2,128,512]{3,2,1,0:T(8,128)(2,1)S(1)}, u32[]{:S(2)}, u32[]{:S(2)}) collective-permute-start(bf16[2,2,128,512]{3,2,1,0:T(8,128)(2,1)S(1)} %bitcast.254), channel_id=1, source_target_pairs={{0,12},{4,8},{8,4},{12,0},{16,28},{20,24},{24,20},{28,16},{1,13},{... | collective-permute-start | bytes 1572872 | tf_op jit(solution)/shard_map/ppermute | solution.py:55
  141.4 9.5 %collective-permute-start.27 = (bf16[512,1024]{1,0:T(8,128)(2,1)S(1)}, bf16[512,1024]{1,0:T(8,128)(2,1)S(1)}, u32[]{:S(2)}, u32[]{:S(2)}) collective-permute-start(bf16[512,1024]{1,0:T(8,128)(2,1)S(1)} %convolution_convert_fusion.3), channel_id=1, source_target_pairs={{0,32},{32,0},{64,96},{96,64},{1,33},{33,1},{65,97},{97,65},{2,34}... | collective-permute-start | bytes 3145736 | tf_op jit(solution)/shard_map/ppermute | solution.py:63
  154.9 12.1 %collective-permute-start.32 = (bf16[512,384]{1,0:T(8,128)(2,1)S(1)}, bf16[512,384]{1,0:T(8,128)(2,1)S(1)}, u32[]{:S(2)}, u32[]{:S(2)}) collective-permute-start(bf16[512,384]{1,0:T(8,128)(2,1)S(1)} %pad_maximum_fusion.25), channel_id=1, source_target_pairs={{0,1},{1,0},{2,3},{3,2},{4,5},{5,4},{6,7},{7,6},{8,9},{9,8},{10,11... | collective-permute-start | bytes 1179656 | tf_op jit(solution)/shard_map/ppermute | solution.py:59
  156.5 20.4 %collective-permute-start.33 = (bf16[512,384]{1,0:T(8,128)(2,1)S(1)}, bf16[512,384]{1,0:T(8,128)(2,1)S(1)}, u32[]{:S(2)}, u32[]{:S(2)}) collective-permute-start(bf16[512,384]{1,0:T(8,128)(2,1)S(1)} %pad_maximum_fusion.26), channel_id=1, source_target_pairs={{0,3},{1,2},{2,1},{3,0},{4,7},{5,6},{6,5},{7,4},{8,11},{9,10},{10,... | collective-permute-start | bytes 1179656 | tf_op jit(solution)/shard_map/ppermute | solution.py:59
  157.9 19.1 %collective-permute-start.34 = (bf16[512,384]{1,0:T(8,128)(2,1)S(1)}, bf16[512,384]{1,0:T(8,128)(2,1)S(1)}, u32[]{:S(2)}, u32[]{:S(2)}) collective-permute-start(bf16[512,384]{1,0:T(8,128)(2,1)S(1)} %pad_maximum_fusion.27), channel_id=1, source_target_pairs={{0,2},{1,3},{2,0},{3,1},{4,6},{5,7},{6,4},{7,5},{8,10},{9,11},{10,... | collective-permute-start | bytes 1179656 | tf_op jit(solution)/shard_map/ppermute | solution.py:59
  (42 other events, 163.6 us)
where the time goes:
time: 187 us
  waiting for transfers between devices  88.2 us (47%)
  starting transfers between devices  44.4 us (24%)
  matrix products  19.7 us (11%)
  local copies, waits for them, and re-layouts  18.1 us (10%)
  other arithmetic  13.6 us (7%)
  between operations  2.55 us (1%)
    ppermute x21, waiting for transfers between devices, over_gy(): return lax.ppermute(block, 'gy', GY_PAIRS[bit])  60.9 us
    ppermute x21, starting transfers between devices, over_gy(): return lax.ppermute(block, 'gy', GY_PAIRS[bit])  23.6 us
    ppermute x9, waiting for transfers between devices, over_gz(): return lax.ppermute(block, 'gz', GZ_PAIRS[step])  20.5 us
    ppermute x9, starting transfers between devices, over_gz(): return lax.ppermute(block, 'gz', GZ_PAIRS[step])  14.5 us
    unnamed x75, local copies, waits for them, and re-layouts  8.86 us
    ppermute x2, waiting for transfers between devices, over_high(): return lax.ppermute(block, 'gx', HIGH_PAIRS)  6.77 us
    dot_general x2, matrix products, dot_tn(): lax.dot_general(left, right, (((0,), (0,)), ((), ())), preferred_element_...  6.7 us
    dot_general x3, matrix products, dot_nn(): lax.dot_general(left, right, (((1,), (0,)), ((), ())), preferred_element_...  6.52 us
  transfers between devices with their start and end apart: 36, of which 22 were waited for; matrix products, arithmetic and copies ran while one was open for 18% of the time, Pallas kernels for 0%

commit v1 on v0

--- a/solution.py
+++ b/solution.py
@@ -128,14 +128,14 @@
         )
         held = add(held, over_gy(away, first)).astype(bf16)
         held = add(pick(held, axis, 0), over_gy(pick(held, axis, 1), second)).astype(bf16)
-        if not cubes[0]:
-            begun = held
         total = add(held[:, 0], over_gy(held[:, 1], third))
         active = gelu_value(total[0]).astype(bf16)
         grad = (total[1] * gelu_slope(total[0])).astype(bf16)
         piece = jnp.stack([active, grad])
         pair = jnp.stack([piece, over_gy(piece, third)], axis=1)
         square = jnp.stack([pair, over_gy(pair, second)], axis=1)
+        if not cubes[0]:
+            begun = pair
         axes = [(first, second, third).index(bit) for bit in (2, 1, 0)]
         for side, full in zip(square, cubes):
             cube = jnp.stack([side, over_gy(side, first)])
@@ -171,15 +171,19 @@
         left, right = (side[:, p * slot : (p + 1) * slot] for side in (out_mine, grad_mine))
         return jnp.concatenate([left[:, :lap], left[:, lap:] + right[:, :lap], right[:, lap:]], axis=1)
 
-    got = [over_gz(joined(step), step) for step in (1, 2, 3)]
+    pieces = [joined(p).reshape(8, 2, rows, 3 * lap) for p in range(4)]
+    orders = ((1, 2), (2, 1))
+    got = [over_gz(jnp.stack([pieces[f][:, h], pieces[3][:, h]]), f) for h, (f, s) in enumerate(orders)]
     features, grad_feats = gate([features, grad_feats], [out_mine, grad_mine])
     grad_weight_out = dot_tn(active_rows.reshape(-1, hidden), grad_feats.reshape(-1, depth)).astype(bf16)
     grad_weight_in = dot_tn(features.reshape(-1, depth), grad_rows.reshape(-1, hidden)).astype(bf16)
-    total = joined(0).astype(f32)
-    for block in gate(got, [grad_weight_out, grad_weight_in]):
-        total += block.astype(f32)
-    total = total.reshape(8, 2, rows, 3 * lap)
-    total = add(total[:, 0], over_high(total[:, 1].astype(bf16))).astype(bf16)
+    got = gate(got, [grad_weight_out])
+    near = [
+        add(jnp.stack([pieces[0][:, h], pieces[s][:, h]]), got[h]).astype(bf16) for h, (f, s) in enumerate(orders)
+    ]
+    got = gate([over_gz(near[h][1], s) for h, (f, s) in enumerate(orders)], [grad_weight_in])
+    total = [add(side[0], block) for side, block in zip(near, got)]
+    total = add(total[0], over_high(total[1].astype(bf16))).astype(bf16)
     total = jnp.concatenate([dyn(total, p ^ gy_id) for p in range(8)], axis=0)
     return (total[:, :width], total[:, -width:], grad_weight_in, grad_weight_out)
 

time: 187 us -> 185 us (0.989)
  waiting for transfers between devices: 88.2 us -> 82.8 us
  other arithmetic: 13.6 us -> 17.5 us
  local copies, waits for them, and re-layouts: 18.1 us -> 15.2 us
  starting transfers between devices: 44.4 us -> 46.9 us
    ppermute x21, waiting for transfers between devices: 60.9 us -> 55.7 us  [over_gy(): return lax.ppermute(block, 'gy', GY_PAIRS[bit])]
    ppermute x21, starting transfers between devices: 23.6 us -> 26.8 us  [over_gy(): return lax.ppermute(block, 'gy', GY_PAIRS[bit])]
    another operation x6, other arithmetic: 0.48 us -> 3.33 us  [per_device(): square = jnp.stack([pair, over_gy(pair, second)], axis=1)]
    another operation x3, other arithmetic: 0.11 us -> 2.42 us  [per_device(): pair = jnp.stack([piece, over_gy(piece, third)], axis=1)]
    unnamed x75 -> x84, local copies, waits for them, and re-layouts: 8.86 us -> 10.4 us
    ppermute x9 -> x10, waiting for transfers between devices: 20.5 us -> 19.4 us  [over_gz(): return lax.ppermute(block, 'gz', GZ_PAIRS[step])]
    ppermute x9 -> x10, starting transfers between devices: 14.5 us -> 14.5 us  [over_gz(): return lax.ppermute(block, 'gz', GZ_PAIRS[step])]
  transfers between devices with their start and end apart: 36 -> 37, of which waited for: 22 -> 24; matrix products, arithmetic and copies ran while one was open for 18% -> 19% of each run, Pallas kernels for 0% -> 0%
where the time goes in v1:
time: 185 us
  waiting for transfers between devices  82.8 us (45%)
  starting transfers between devices  46.9 us (25%)
  matrix products  19.7 us (11%)
  other arithmetic  17.5 us (9%)
  local copies, waits for them, and re-layouts  15.2 us (8%)
  between operations  2.62 us (1%)
    ppermute x21, waiting for transfers between devices, over_gy(): return lax.ppermute(block, 'gy', GY_PAIRS[bit])  55.7 us
    ppermute x21, starting transfers between devices, over_gy(): return lax.ppermute(block, 'gy', GY_PAIRS[bit])  26.8 us
    ppermute x10, waiting for transfers between devices, over_gz(): return lax.ppermute(block, 'gz', GZ_PAIRS[step])  19.4 us
    ppermute x10, starting transfers between devices, over_gz(): return lax.ppermute(block, 'gz', GZ_PAIRS[step])  14.5 us
    unnamed x84, local copies, waits for them, and re-layouts  10.4 us
    ppermute x2, waiting for transfers between devices, over_high(): return lax.ppermute(block, 'gx', HIGH_PAIRS)  7.48 us
    dot_general x2, matrix products, dot_tn(): lax.dot_general(left, right, (((0,), (0,)), ((), ())), preferred_element_...  6.69 us
    dot_general x3, matrix products, dot_nt(): lax.dot_general(left, right, (((1,), (1,)), ((), ())), preferred_element_...  6.51 us
  transfers between devices with their start and end apart: 37, of which 24 were waited for; matrix products, arithmetic and copies ran while one was open for 19% of the time, Pallas kernels for 0%

profile of v1, /device:TPU:0, one launch (start us, length us, event | category | flops | bytes accessed | tf_op | source)
XLA Modules:
  0.0 184.7 jit_solution(13033000260528647104)
XLA Ops:
  3.0 4.0 %collective-permute-start.3 = (bf16[8,32,384]{2,1,0:T(8,128)(2,1)S(1)}, bf16[8,32,384]{2,1,0:T(8,128)(2,1)S(1)}, u32[]{:S(2)}, u32[]{:S(2)}) collective-permute-start(bf16[8,32,384]{2,1,0:T(8,128)(2,1)S(1)} %constant_dynamic-update-slice_fusion), channel_id=1, source_target_pairs={{0,64},{32,96},{64,0},{96,32},{1,65},{33,97},{65,1},{97,33},{2,66}... | collective-permute-start | bytes 589832 | tf_op jit(solution)/shard_map/ppermute | solution.py:67
  7.0 3.0 %collective-permute-start.2 = (bf16[8,32,384]{2,1,0:T(8,128)(2,1)S(1)}, bf16[8,32,384]{2,1,0:T(8,128)(2,1)S(1)}, u32[]{:S(2)}, u32[]{:S(2)}) collective-permute-start(bf16[8,32,384]{2,1,0:T(8,128)(2,1)S(1)} %constant_dynamic-update-slice_fusion), channel_id=1, source_target_pairs={{0,2},{1,3},{2,0},{3,1},{4,6},{5,7},{6,4},{7,5},{8,10},{9,11},{10,... | collective-permute-start | bytes 589832 | tf_op jit(solution)/shard_map/ppermute | solution.py:59
  11.9 3.0 %collective-permute-start.6 = (bf16[8,32,384]{2,1,0:T(8,128)(2,1)S(1)}, bf16[8,32,384]{2,1,0:T(8,128)(2,1)S(1)}, u32[]{:S(2)}, u32[]{:S(2)}) collective-permute-start(bf16[8,32,384]{2,1,0:T(8,128)(2,1)S(1)} %collective-permute-done.3), channel_id=1, source_target_pairs={{0,2},{1,3},{2,0},{3,1},{4,6},{5,7},{6,4},{7,5},{8,10},{9,11},{10,... | collective-permute-start | bytes 589832 | tf_op jit(solution)/shard_map/ppermute | solution.py:59
  17.9 4.4 %collective-permute-done.1 = bf16[8,32,384]{2,1,0:T(8,128)(2,1)S(1)} collective-permute-done((bf16[8,32,384]{2,1,0:T(8,128)(2,1)S(1)}, bf16[8,32,384]{2,1,0:T(8,128)(2,1)S(1)}, u32[]{:S(2)}, u32[]{:S(2)}) %collective-permute-start.1) | collective-permute-done | bytes 196640 | tf_op jit(solution)/shard_map/ppermute | solution.py:59
  22.4 2.4 %collective-permute-done.6 = bf16[8,32,384]{2,1,0:T(8,128)(2,1)S(1)} collective-permute-done((bf16[8,32,384]{2,1,0:T(8,128)(2,1)S(1)}, bf16[8,32,384]{2,1,0:T(8,128)(2,1)S(1)}, u32[]{:S(2)}, u32[]{:S(2)}) %collective-permute-start.6) | collective-permute-done | bytes 196640 | tf_op jit(solution)/shard_map/ppermute | solution.py:59
  24.8 2.7 %collective-permute-done.5 = bf16[8,32,384]{2,1,0:T(8,128)(2,1)S(1)} collective-permute-done((bf16[8,32,384]{2,1,0:T(8,128)(2,1)S(1)}, bf16[8,32,384]{2,1,0:T(8,128)(2,1)S(1)}, u32[]{:S(2)}, u32[]{:S(2)}) %collective-permute-start.5) | collective-permute-done | bytes 196640 | tf_op jit(solution)/shard_map/ppermute | solution.py:59
  34.0 2.9 %convolution_convert_fusion = bf16[1024,1536]{1,0:T(8,128)(2,1)S(1)} fusion(bf16[1024,768]{1,0:T(8,128)(2,1)S(1)} %bitcast.306, bf16[1536,768]{1,0:T(8,128)(2,1)S(1)} %copy-done.2), kind=kOutput, calls=%fused_computation.26 | convolution fusion | flops 2417491968 | bytes 7077888 | tf_op jit(solution)/shard_map/dot_general | solution.py:33
  38.9 2.8 %convolution_convert_fusion.1 = bf16[1024,1536]{1,0:T(8,128)(2,1)S(1)} fusion(bf16[1024,768]{1,0:T(8,128)(2,1)S(1)} %bitcast.307, bf16[768,1536]{1,0:T(8,128)(2,1)S(1)} %copy-done.3), kind=kOutput, calls=%fused_computation.27 | convolution fusion | flops 2417491968 | bytes 7077888 | tf_op jit(solution)/shard_map/dot_general | solution.py:25
  45.2 2.3 %collective-permute-start.15 = (bf16[2,2,2,128,512]{4,3,0,1,2:T(8,128)(2,1)S(1)}, bf16[2,2,2,128,512]{4,3,0,1,2:T(8,128)(2,1)S(1)}, u32[]{:S(2)}, u32[]{:S(2)}) collective-permute-start(bf16[2,2,2,128,512]{4,3,0,1,2:T(8,128)(2,1)S(1)} %pad_maximum_fusion.7), channel_id=1, source_target_pairs={{0,12},{4,8},{8,4},{12,0},{16,28},{20,24},{24,20},{28,16},{1,13},{... | collective-permute-start | bytes 3145736 | tf_op jit(solution)/shard_map/ppermute | solution.py:55
  47.6 19.6 %collective-permute-done.21 = bf16[2,2,2,128,512]{4,3,2,1,0:T(8,128)(2,1)S(1)} collective-permute-done((bf16[2,2,2,128,512]{4,3,2,1,0:T(8,128)(2,1)S(1)}, bf16[2,2,2,128,512]{4,3,2,1,0:T(8,128)(2,1)S(1)}, u32[]{:S(2)}, u32[]{:S(2)}) %collective-permute-start.21) | collective-permute-done | bytes 1048608 | tf_op jit(solution)/shard_map/ppermute | solution.py:55
  69.1 3.0 %collective-permute-start.10 = (bf16[2,2,128,512]{3,2,0,1:T(8,128)(2,1)S(1)}, bf16[2,2,128,512]{3,2,0,1:T(8,128)(2,1)S(1)}, u32[]{:S(2)}, u32[]{:S(2)}) collective-permute-start(bf16[2,2,128,512]{3,2,0,1:T(8,128)(2,1)S(1)} %slice_bitcast_fusion.8), channel_id=1, source_target_pairs={{0,12},{4,8},{8,4},{12,0},{16,28},{20,24},{24,20},{28,16},{1,13},{... | collective-permute-start | bytes 1572872 | tf_op jit(solution)/shard_map/ppermute | solution.py:55
  72.7 8.0 %collective-permute-done.22 = bf16[2,2,128,512]{3,2,1,0:T(8,128)(2,1)S(1)} collective-permute-done((bf16[2,2,128,512]{3,2,1,0:T(8,128)(2,1)S(1)}, bf16[2,2,128,512]{3,2,1,0:T(8,128)(2,1)S(1)}, u32[]{:S(2)}, u32[]{:S(2)}) %collective-permute-start.22) | collective-permute-done | bytes 524320 | tf_op jit(solution)/shard_map/ppermute | solution.py:55
  81.7 3.0 %collective-permute-start.23 = (bf16[2,128,512]{2,1,0:T(8,128)(2,1)}, bf16[2,128,512]{2,1,0:T(8,128)(2,1)}, u32[]{:S(2)}, u32[]{:S(2)}) collective-permute-start(bf16[2,128,512]{2,1,0:T(8,128)(2,1)} %slice_bitcast_fusion.14), channel_id=1, source_target_pairs={{0,12},{4,8},{8,4},{12,0},{16,28},{20,24},{24,20},{28,16},{1,13},{... | collective-permute-start | bytes 786440 | tf_op jit(solution)/shard_map/ppermute | solution.py:55
  87.1 4.2 %collective-permute-done.11 = bf16[2,128,512]{2,1,0:T(8,128)(2,1)S(1)} collective-permute-done((bf16[2,128,512]{2,1,0:T(8,128)(2,1)S(1)}, bf16[2,128,512]{2,1,0:T(8,128)(2,1)S(1)}, u32[]{:S(2)}, u32[]{:S(2)}) %collective-permute-start.11) | collective-permute-done | bytes 262176 | tf_op jit(solution)/shard_map/ppermute | solution.py:55
  113.0 4.7 %collective-permute-done.25 = bf16[2,2,128,512]{3,2,0,1:T(8,128)(2,1)S(1)} collective-permute-done((bf16[2,2,128,512]{3,2,0,1:T(8,128)(2,1)S(1)}, bf16[2,2,128,512]{3,2,0,1:T(8,128)(2,1)S(1)}, u32[]{:S(2)}, u32[]{:S(2)}) %collective-permute-start.25) | collective-permute-done | bytes 524320 | tf_op jit(solution)/shard_map/ppermute | solution.py:55
  121.8 3.4 %collective-permute-done.13 = bf16[2,2,128,512]{3,2,0,1:T(8,128)(2,1)S(1)} collective-permute-done((bf16[2,2,128,512]{3,2,0,1:T(8,128)(2,1)S(1)}, bf16[2,2,128,512]{3,2,0,1:T(8,128)(2,1)S(1)}, u32[]{:S(2)}, u32[]{:S(2)}) %collective-permute-start.13) | collective-permute-done | bytes 524320 | tf_op jit(solution)/shard_map/ppermute | solution.py:55
  128.6 7.8 %collective-permute-done.20 = bf16[2,2,128,512]{3,2,1,0:T(8,128)(2,1)S(1)} collective-permute-done((bf16[2,2,128,512]{3,2,1,0:T(8,128)(2,1)S(1)}, bf16[2,2,128,512]{3,2,1,0:T(8,128)(2,1)S(1)}, u32[]{:S(2)}, u32[]{:S(2)}) %collective-permute-start.20) | collective-permute-done | bytes 524320 | tf_op jit(solution)/shard_map/ppermute | solution.py:55
  140.2 4.4 %collective-permute-done.29 = bf16[2,2,128,512]{3,2,1,0:T(8,128)(2,1)S(1)} collective-permute-done((bf16[2,2,128,512]{3,2,1,0:T(8,128)(2,1)S(1)}, bf16[2,2,128,512]{3,2,1,0:T(8,128)(2,1)S(1)}, u32[]{:S(2)}, u32[]{:S(2)}) %collective-permute-start.29) | collective-permute-done | bytes 524320 | tf_op jit(solution)/shard_map/ppermute | solution.py:55
  157.0 3.5 %bitcast_convert_fusion.1.refs_2_ = bf16[1536,768]{1,0:T(8,128)(2,1)S(1)} fusion(bf16[2,2,2,2,2,32,768]{6,5,4,3,2,1,0:T(8,128)(2,1)S(1)} %get-tuple-element.10, bf16[2,2,2,2,2,32,512]{6,5,4,3,2,1,0:T(8,128)(2,1)S(1)} %bitcast.277, bf16[2,2,2,2,2,32,512]{6,5,4,3,2,1,0:T(8,128)(2,1)S(1)} %bitcast.275, bf16[1,2,2,2,2,32,512]{6,5,4,3,2,1,0:T(8,128)(2,1)S(1)} %bitcast.327, ...), kind=kOutput, calls=%fused_computation.25 | convolution fusion | flops 2429681664 | bytes 7077888 | tf_op jit(solution)/shard_map/dot_general | solution.py:29
  160.7 4.6 %collective-permute-done.32.refs_0_ = bf16[2,8,32,384]{3,2,1,0:T(8,128)(2,1)S(1)} collective-permute-done((bf16[2,8,32,384]{3,2,1,0:T(8,128)(2,1)S(1)}, bf16[2,8,32,384]{3,2,1,0:T(8,128)(2,1)S(1)}, u32[]{:S(2)}, u32[]{:S(2)}) %collective-permute-start.32) | collective-permute-done | bytes 393248 | tf_op jit(solution)/shard_map/ppermute | solution.py:59
  165.3 2.6 %collective-permute-done.33.refs_1_ = bf16[2,8,32,384]{3,2,1,0:T(8,128)(2,1)S(1)} collective-permute-done((bf16[2,8,32,384]{3,2,1,0:T(8,128)(2,1)S(1)}, bf16[2,8,32,384]{3,2,1,0:T(8,128)(2,1)S(1)}, u32[]{:S(2)}, u32[]{:S(2)}) %collective-permute-start.33) | collective-permute-done | bytes 393248 | tf_op jit(solution)/shard_map/ppermute | solution.py:59
  169.8 3.2 %bitcast_convert_fusion.refs_2_ = bf16[768,1536]{1,0:T(8,128)(2,1)S(1)} fusion(bf16[2,2,2,2,2,32,768]{6,5,4,3,2,1,0:T(8,128)(2,1)S(1)} %get-tuple-element.13, bf16[2,2,2,2,2,32,512]{6,5,4,3,2,1,0:T(8,128)(2,1)S(1)} %bitcast.273, bf16[2,2,2,2,2,32,512]{6,5,4,3,2,1,0:T(8,128)(2,1)S(1)} %bitcast.271, bf16[1,2,2,2,2,32,512]{6,5,4,3,2,1,0:T(8,128)(2,1)S(1)} %bitcast.325, ...), kind=kOutput, calls=%fused_computation.24 | convolution fusion | flops 2429681664 | bytes 7077888 | tf_op jit(solution)/shard_map/dot_general | solution.py:29
  173.0 2.0 %collective-permute-done.34.refs_0_ = bf16[8,32,384]{2,1,0:T(8,128)(2,1)S(1)} collective-permute-done((bf16[8,32,384]{2,1,0:T(8,128)(2,1)S(1)}, bf16[8,32,384]{2,1,0:T(8,128)(2,1)S(1)}, u32[]{:S(2)}, u32[]{:S(2)}) %collective-permute-start.34) | collective-permute-done | bytes 196640 | tf_op jit(solution)/shard_map/ppermute | solution.py:59
  176.1 6.7 %collective-permute-done.36 = bf16[8,32,384]{2,1,0:T(8,128)(2,1)S(1)} collective-permute-done((bf16[8,32,384]{2,1,0:T(8,128)(2,1)S(1)}, bf16[8,32,384]{2,1,0:T(8,128)(2,1)S(1)}, u32[]{:S(2)}, u32[]{:S(2)}) %collective-permute-start.36) | collective-permute-done | bytes 196640 | tf_op jit(solution)/shard_map/ppermute | solution.py:67
  (244 shorter events, 73.6 us)
Async XLA Ops:
  10.0 12.2 %collective-permute-start.1 = (bf16[8,32,384]{2,1,0:T(8,128)(2,1)S(1)}, bf16[8,32,384]{2,1,0:T(8,128)(2,1)S(1)}, u32[]{:S(2)}, u32[]{:S(2)}) collective-permute-start(bf16[8,32,384]{2,1,0:T(8,128)(2,1)S(1)} %constant_dynamic-update-slice_fusion), channel_id=1, source_target_pairs={{0,3},{1,2},{2,1},{3,0},{4,7},{5,6},{6,5},{7,4},{8,11},{9,10},{10,... | collective-permute-start | bytes 589832 | tf_op jit(solution)/shard_map/ppermute | solution.py:59
  11.2 11.1 %collective-permute-start = (bf16[8,32,384]{2,1,0:T(8,128)(2,1)S(1)}, bf16[8,32,384]{2,1,0:T(8,128)(2,1)S(1)}, u32[]{:S(2)}, u32[]{:S(2)}) collective-permute-start(bf16[8,32,384]{2,1,0:T(8,128)(2,1)S(1)} %constant_dynamic-update-slice_fusion), channel_id=1, source_target_pairs={{0,1},{1,0},{2,3},{3,2},{4,5},{5,4},{6,7},{7,6},{8,9},{9,8},{10,11... | collective-permute-start | bytes 589832 | tf_op jit(solution)/shard_map/ppermute | solution.py:59
  11.9 12.9 %collective-permute-start.6 = (bf16[8,32,384]{2,1,0:T(8,128)(2,1)S(1)}, bf16[8,32,384]{2,1,0:T(8,128)(2,1)S(1)}, u32[]{:S(2)}, u32[]{:S(2)}) collective-permute-start(bf16[8,32,384]{2,1,0:T(8,128)(2,1)S(1)} %collective-permute-done.3), channel_id=1, source_target_pairs={{0,2},{1,3},{2,0},{3,1},{4,6},{5,7},{6,4},{7,5},{8,10},{9,11},{10,... | collective-permute-start | bytes 589832 | tf_op jit(solution)/shard_map/ppermute | solution.py:59
  14.9 12.6 %collective-permute-start.5 = (bf16[8,32,384]{2,1,0:T(8,128)(2,1)S(1)}, bf16[8,32,384]{2,1,0:T(8,128)(2,1)S(1)}, u32[]{:S(2)}, u32[]{:S(2)}) collective-permute-start(bf16[8,32,384]{2,1,0:T(8,128)(2,1)S(1)} %collective-permute-done.3), channel_id=1, source_target_pairs={{0,3},{1,2},{2,1},{3,0},{4,7},{5,6},{6,5},{7,4},{8,11},{9,10},{10,... | collective-permute-start | bytes 589832 | tf_op jit(solution)/shard_map/ppermute | solution.py:59
  16.1 11.6 %collective-permute-start.4 = (bf16[8,32,384]{2,1,0:T(8,128)(2,1)S(1)}, bf16[8,32,384]{2,1,0:T(8,128)(2,1)S(1)}, u32[]{:S(2)}, u32[]{:S(2)}) collective-permute-start(bf16[8,32,384]{2,1,0:T(8,128)(2,1)S(1)} %collective-permute-done.3), channel_id=1, source_target_pairs={{0,1},{1,0},{2,3},{3,2},{4,5},{5,4},{6,7},{7,6},{8,9},{9,8},{10,11... | collective-permute-start | bytes 589832 | tf_op jit(solution)/shard_map/ppermute | solution.py:59
  41.9 25.3 %collective-permute-start.21 = (bf16[2,2,2,128,512]{4,3,2,1,0:T(8,128)(2,1)S(1)}, bf16[2,2,2,128,512]{4,3,2,1,0:T(8,128)(2,1)S(1)}, u32[]{:S(2)}, u32[]{:S(2)}) collective-permute-start(bf16[2,2,2,128,512]{4,3,2,1,0:T(8,128)(2,1)S(1)} %pad_maximum_fusion.8), channel_id=1, source_target_pairs={{0,4},{4,0},{8,12},{12,8},{16,20},{20,16},{24,28},{28,24},{1,5},{5... | collective-permute-start | bytes 3145736 | tf_op jit(solution)/shard_map/ppermute | solution.py:55
  43.8 25.0 %collective-permute-start.9 = (bf16[2,2,2,128,512]{4,3,0,2,1:T(8,128)(2,1)S(1)}, bf16[2,2,2,128,512]{4,3,0,2,1:T(8,128)(2,1)S(1)}, u32[]{:S(2)}, u32[]{:S(2)}) collective-permute-start(bf16[2,2,2,128,512]{4,3,0,2,1:T(8,128)(2,1)S(1)} %pad_maximum_fusion.6), channel_id=1, source_target_pairs={{0,16},{4,20},{8,24},{12,28},{16,0},{20,4},{24,8},{28,12},{1,17},{... | collective-permute-start | bytes 3145736 | tf_op jit(solution)/shard_map/ppermute | solution.py:55
  45.2 26.9 %collective-permute-start.15 = (bf16[2,2,2,128,512]{4,3,0,1,2:T(8,128)(2,1)S(1)}, bf16[2,2,2,128,512]{4,3,0,1,2:T(8,128)(2,1)S(1)}, u32[]{:S(2)}, u32[]{:S(2)}) collective-permute-start(bf16[2,2,2,128,512]{4,3,0,1,2:T(8,128)(2,1)S(1)} %pad_maximum_fusion.7), channel_id=1, source_target_pairs={{0,12},{4,8},{8,4},{12,0},{16,28},{20,24},{24,20},{28,16},{1,13},{... | collective-permute-start | bytes 3145736 | tf_op jit(solution)/shard_map/ppermute | solution.py:55
  67.5 13.2 %collective-permute-start.22 = (bf16[2,2,128,512]{3,2,1,0:T(8,128)(2,1)S(1)}, bf16[2,2,128,512]{3,2,1,0:T(8,128)(2,1)S(1)}, u32[]{:S(2)}, u32[]{:S(2)}) collective-permute-start(bf16[2,2,128,512]{3,2,1,0:T(8,128)(2,1)S(1)} %slice_bitcast_fusion), channel_id=1, source_target_pairs={{0,16},{4,20},{8,24},{12,28},{16,0},{20,4},{24,8},{28,12},{1,17},{... | collective-permute-start | bytes 1572872 | tf_op jit(solution)/shard_map/ppermute | solution.py:55
  69.1 15.6 %collective-permute-start.10 = (bf16[2,2,128,512]{3,2,0,1:T(8,128)(2,1)S(1)}, bf16[2,2,128,512]{3,2,0,1:T(8,128)(2,1)S(1)}, u32[]{:S(2)}, u32[]{:S(2)}) collective-permute-start(bf16[2,2,128,512]{3,2,0,1:T(8,128)(2,1)S(1)} %slice_bitcast_fusion.8), channel_id=1, source_target_pairs={{0,12},{4,8},{8,4},{12,0},{16,28},{20,24},{24,20},{28,16},{1,13},{... | collective-permute-start | bytes 1572872 | tf_op jit(solution)/shard_map/ppermute | solution.py:55
  72.5 12.7 %collective-permute-start.16 = (bf16[2,2,128,512]{3,2,0,1:T(8,128)(2,1)S(1)}, bf16[2,2,128,512]{3,2,0,1:T(8,128)(2,1)S(1)}, u32[]{:S(2)}, u32[]{:S(2)}) collective-permute-start(bf16[2,2,128,512]{3,2,0,1:T(8,128)(2,1)S(1)} %slice_bitcast_fusion.6), channel_id=1, source_target_pairs={{0,4},{4,0},{8,12},{12,8},{16,20},{20,16},{24,28},{28,24},{1,5},{5... | collective-permute-start | bytes 1572872 | tf_op jit(solution)/shard_map/ppermute | solution.py:55
  81.7 12.5 %collective-permute-start.23 = (bf16[2,128,512]{2,1,0:T(8,128)(2,1)}, bf16[2,128,512]{2,1,0:T(8,128)(2,1)}, u32[]{:S(2)}, u32[]{:S(2)}) collective-permute-start(bf16[2,128,512]{2,1,0:T(8,128)(2,1)} %slice_bitcast_fusion.14), channel_id=1, source_target_pairs={{0,12},{4,8},{8,4},{12,0},{16,28},{20,24},{24,20},{28,16},{1,13},{... | collective-permute-start | bytes 786440 | tf_op jit(solution)/shard_map/ppermute | solution.py:55
  86.1 11.7 %collective-permute-start.17 = (bf16[2,128,512]{2,1,0:T(8,128)(2,1)}, bf16[2,128,512]{2,1,0:T(8,128)(2,1)}, u32[]{:S(2)}, u32[]{:S(2)}) collective-permute-start(bf16[2,128,512]{2,1,0:T(8,128)(2,1)} %slice_bitcast_fusion.16), channel_id=1, source_target_pairs={{0,16},{4,20},{8,24},{12,28},{16,0},{20,4},{24,8},{28,12},{1,17},{... | collective-permute-start | bytes 786440 | tf_op jit(solution)/shard_map/ppermute | solution.py:55
  105.8 12.0 %collective-permute-start.25 = (bf16[2,2,128,512]{3,2,0,1:T(8,128)(2,1)S(1)}, bf16[2,2,128,512]{3,2,0,1:T(8,128)(2,1)S(1)}, u32[]{:S(2)}, u32[]{:S(2)}) collective-permute-start(bf16[2,2,128,512]{3,2,0,1:T(8,128)(2,1)S(1)} %get-tuple-element.85), channel_id=1, source_target_pairs={{0,16},{4,20},{8,24},{12,28},{16,0},{20,4},{24,8},{28,12},{1,17},{... | collective-permute-start | bytes 1572872 | tf_op jit(solution)/shard_map/ppermute | solution.py:55
  108.8 11.0 %collective-permute-start.19 = (bf16[2,2,128,512]{3,2,0,1:T(8,128)(2,1)S(1)}, bf16[2,2,128,512]{3,2,0,1:T(8,128)(2,1)S(1)}, u32[]{:S(2)}, u32[]{:S(2)}) collective-permute-start(bf16[2,2,128,512]{3,2,0,1:T(8,128)(2,1)S(1)} %get-tuple-element.81), channel_id=1, source_target_pairs={{0,4},{4,0},{8,12},{12,8},{16,20},{20,16},{24,28},{28,24},{1,5},{5... | collective-permute-start | bytes 1572872 | tf_op jit(solution)/shard_map/ppermute | solution.py:55
  111.0 14.1 %collective-permute-start.13 = (bf16[2,2,128,512]{3,2,0,1:T(8,128)(2,1)S(1)}, bf16[2,2,128,512]{3,2,0,1:T(8,128)(2,1)S(1)}, u32[]{:S(2)}, u32[]{:S(2)}) collective-permute-start(bf16[2,2,128,512]{3,2,0,1:T(8,128)(2,1)S(1)} %get-tuple-element.77), channel_id=1, source_target_pairs={{0,12},{4,8},{8,4},{12,0},{16,28},{20,24},{24,20},{28,16},{1,13},{... | collective-permute-start | bytes 1572872 | tf_op jit(solution)/shard_map/ppermute | solution.py:55
  117.8 19.8 %collective-permute-start.26 = (bf16[2,2,128,512]{3,2,1,0:T(8,128)(2,1)S(1)}, bf16[2,2,128,512]{3,2,1,0:T(8,128)(2,1)S(1)}, u32[]{:S(2)}, u32[]{:S(2)}) collective-permute-start(bf16[2,2,128,512]{3,2,1,0:T(8,128)(2,1)S(1)} %bitcast.300), channel_id=1, source_target_pairs={{0,4},{4,0},{8,12},{12,8},{16,20},{20,16},{24,28},{28,24},{1,5},{5... | collective-permute-start | bytes 1572872 | tf_op jit(solution)/shard_map/ppermute | solution.py:55
  119.8 16.6 %collective-permute-start.20 = (bf16[2,2,128,512]{3,2,1,0:T(8,128)(2,1)S(1)}, bf16[2,2,128,512]{3,2,1,0:T(8,128)(2,1)S(1)}, u32[]{:S(2)}, u32[]{:S(2)}) collective-permute-start(bf16[2,2,128,512]{3,2,1,0:T(8,128)(2,1)S(1)} %bitcast.301), channel_id=1, source_target_pairs={{0,12},{4,8},{8,4},{12,0},{16,28},{20,24},{24,20},{28,16},{1,13},{... | collective-permute-start | bytes 1572872 | tf_op jit(solution)/shard_map/ppermute | solution.py:55
  125.3 12.5 %collective-permute-start.14 = (bf16[2,2,128,512]{3,2,1,0:T(8,128)(2,1)S(1)}, bf16[2,2,128,512]{3,2,1,0:T(8,128)(2,1)S(1)}, u32[]{:S(2)}, u32[]{:S(2)}) collective-permute-start(bf16[2,2,128,512]{3,2,1,0:T(8,128)(2,1)S(1)} %bitcast.291), channel_id=1, source_target_pairs={{0,16},{4,20},{8,24},{12,28},{16,0},{20,4},{24,8},{28,12},{1,17},{... | collective-permute-start | bytes 1572872 | tf_op jit(solution)/shard_map/ppermute | solution.py:55
  126.6 18.2 %collective-permute-start.30 = (bf16[2,2,128,512]{3,2,1,0:T(8,128)(2,1)S(1)}, bf16[2,2,128,512]{3,2,1,0:T(8,128)(2,1)S(1)}, u32[]{:S(2)}, u32[]{:S(2)}) collective-permute-start(bf16[2,2,128,512]{3,2,1,0:T(8,128)(2,1)S(1)} %bitcast.298), channel_id=1, source_target_pairs={{0,4},{4,0},{8,12},{12,8},{16,20},{20,16},{24,28},{28,24},{1,5},{5... | collective-permute-start | bytes 1572872 | tf_op jit(solution)/shard_map/ppermute | solution.py:55
  126.7 17.9 %collective-permute-start.29 = (bf16[2,2,128,512]{3,2,1,0:T(8,128)(2,1)S(1)}, bf16[2,2,128,512]{3,2,1,0:T(8,128)(2,1)S(1)}, u32[]{:S(2)}, u32[]{:S(2)}) collective-permute-start(bf16[2,2,128,512]{3,2,1,0:T(8,128)(2,1)S(1)} %bitcast.299), channel_id=1, source_target_pairs={{0,12},{4,8},{8,4},{12,0},{16,28},{20,24},{24,20},{28,16},{1,13},{... | collective-permute-start | bytes 1572872 | tf_op jit(solution)/shard_map/ppermute | solution.py:55
  140.1 9.8 %collective-permute-start.27 = (bf16[512,1024]{1,0:T(8,128)(2,1)S(1)}, bf16[512,1024]{1,0:T(8,128)(2,1)S(1)}, u32[]{:S(2)}, u32[]{:S(2)}) collective-permute-start(bf16[512,1024]{1,0:T(8,128)(2,1)S(1)} %convolution_convert_fusion.3), channel_id=1, source_target_pairs={{0,32},{32,0},{64,96},{96,64},{1,33},{33,1},{65,97},{97,65},{2,34}... | collective-permute-start | bytes 3145736 | tf_op jit(solution)/shard_map/ppermute | solution.py:63
  154.1 11.2 %collective-permute-start.32 = (bf16[2,8,32,384]{3,2,1,0:T(8,128)(2,1)S(1)}, bf16[2,8,32,384]{3,2,1,0:T(8,128)(2,1)S(1)}, u32[]{:S(2)}, u32[]{:S(2)}) collective-permute-start(bf16[2,8,32,384]{3,2,1,0:T(8,128)(2,1)S(1)} %pad_maximum_fusion.29), channel_id=1, source_target_pairs={{0,1},{1,0},{2,3},{3,2},{4,5},{5,4},{6,7},{7,6},{8,9},{9,8},{10,11... | collective-permute-start | bytes 1179656 | tf_op jit(solution)/shard_map/ppermute | solution.py:59
  155.8 12.1 %collective-permute-start.33 = (bf16[2,8,32,384]{3,2,1,0:T(8,128)(2,1)S(1)}, bf16[2,8,32,384]{3,2,1,0:T(8,128)(2,1)S(1)}, u32[]{:S(2)}, u32[]{:S(2)}) collective-permute-start(bf16[2,8,32,384]{3,2,1,0:T(8,128)(2,1)S(1)} %pad_maximum_fusion.30), channel_id=1, source_target_pairs={{0,3},{1,2},{2,1},{3,0},{4,7},{5,6},{6,5},{7,4},{8,11},{9,10},{10,... | collective-permute-start | bytes 1179656 | tf_op jit(solution)/shard_map/ppermute | solution.py:59
  (43 other events, 172.4 us)

commit v2 on v1

--- a/solution.py
+++ b/solution.py
@@ -105,28 +105,37 @@
 
     both = jnp.concatenate([tokens, grad_out], axis=1).reshape(8, rows, 2 * width)
     own = jnp.stack([dyn(both, p ^ gy_id) for p in range(8)])
-    squares = [jnp.stack([half] + [over_gz(half, step) for step in (1, 2, 3)]) for half in (own, over_high(own))]
-    squares = [[dyn(square, corner(p) ^ gz_id) for p in range(4)] for square in squares]
-    sides = []
-    for lo in (0, width):
-        spread = [jnp.concatenate([s[..., lo : lo + width] for s in square], axis=-1) for square in squares]
-        mine = jnp.stack(spread, axis=1)
-        sides.append(jnp.stack([mine, over_core(mine)], axis=1).reshape(2, 2, 2, 2, 2, rows, depth))
-    features, grad_feats = sides
+    far = over_high(own)
+    arrived = [[over_gz(half, step) for step in (1, 2, 3)] for half in (own, far)]
+    weights = (lambda u: dot_nn(u, weight_in), lambda u: dot_nt(u, weight_out))
+    sides, terms = [], []
+    for half, got in zip((own, far), arrived):
+        if terms:
+            got = gate(got, terms[0])
+        square = jnp.stack([half, *got])
+        square = [dyn(square, corner(p) ^ gz_id) for p in range(4)]
+        mine = [jnp.concatenate([s[..., lo : lo + width] for s in square], axis=-1) for lo in (0, width)]
+        sides.append([jnp.stack([m, over_core(m)], axis=1).reshape(2, 2, 2, 2 * rows, depth) for m in mine])
+        terms.append(
+            [
+                times(side.reshape(-1, depth)).astype(bf16).reshape(2, 2, 2, 2 * rows, hidden)
+                for times, side in zip(weights, sides[-1])
+            ]
+        )
+    features, grad_feats = (jnp.stack([s[i] for s in sides], axis=3) for i in range(2))
 
     def add(left, right):
         return left.astype(f32) + right.astype(f32)
 
     spans = [(i * part, (i + 1) * part) for i in range(PARTS)]
-    terms = dot_nn(features.reshape(-1, depth), weight_in).astype(bf16).reshape(2, 2, 2, 4 * rows, hidden)
-    grad_terms = dot_nt(grad_feats.reshape(-1, depth), weight_out).astype(bf16).reshape(2, 2, 2, 4 * rows, hidden)
     cubes = ([], [])
     for (lo, hi), (first, second, third) in zip(spans, ORDERS):
         axis = 1 + [bit for bit in (2, 1, 0) if bit != first].index(second)
         away, held = (
-            jnp.stack([pick(side[..., lo:hi], 2 - first, k) for side in (terms, grad_terms)]) for k in (1, 0)
+            jnp.stack([jnp.stack([pick(half[i][..., lo:hi], 2 - first, k) for half in terms], axis=2) for i in range(2)])
+            for k in (1, 0)
         )
-        held = add(held, over_gy(away, first)).astype(bf16)
+        held = add(held, over_gy(away, first)).astype(bf16).reshape(2, 2, 2, 4 * rows, part)
         held = add(pick(held, axis, 0), over_gy(pick(held, axis, 1), second)).astype(bf16)
         total = add(held[:, 0], over_gy(held[:, 1], third))
         active = gelu_value(total[0]).astype(bf16)
@@ -160,8 +169,8 @@
     slots_in = slots([weight_in[p * width : (p + 1) * width] for p in range(4)], 0, (slot - width, 0))
 
     def core_sum(times, full):
-        away = times(full[:, :, :, 1].reshape(-1, hidden)).astype(bf16)
-        return add(times(full[:, :, :, 0].reshape(-1, hidden)), over_core(away)).astype(bf16)
+        away = times(full[:, :, :, :, 1].reshape(-1, hidden)).astype(bf16)
+        return add(times(full[:, :, :, :, 0].reshape(-1, hidden)), over_core(away)).astype(bf16)
 
     out_mine = core_sum(lambda u: dot_nn(u, slots_out), active_rows)
     grad_mine = core_sum(lambda u: dot_nt(u, slots_in), grad_rows)

time: 185 us -> 178 us (0.962)
  waiting for transfers between devices: 82.8 us -> 75.7 us
  local copies, waits for them, and re-layouts: 15.2 us -> 10.6 us
  starting transfers between devices: 46.9 us -> 50.9 us
    unnamed x84 -> x48, local copies, waits for them, and re-layouts: 10.4 us -> 5.39 us
    ppermute x2, waiting for transfers between devices: 7.48 us -> 3.84 us  [over_high(): return lax.ppermute(block, 'gx', HIGH_PAIRS)]
    ppermute x21, waiting for transfers between devices: 55.7 us -> 52.6 us  [over_gy(): return lax.ppermute(block, 'gy', GY_PAIRS[bit])]
    ppermute x21, starting transfers between devices: 26.8 us -> 29.7 us  [over_gy(): return lax.ppermute(block, 'gy', GY_PAIRS[bit])]
    ppermute x2, starting transfers between devices: 4.55 us -> 7.29 us  [over_high(): return lax.ppermute(block, 'gx', HIGH_PAIRS)]
    ppermute x10, starting transfers between devices: 14.5 us -> 12.5 us  [over_gz(): return lax.ppermute(block, 'gz', GZ_PAIRS[step])]
    dot_general x3 -> x4, matrix products: 6.51 us -> 6.46 us  [dot_nt(): lax.dot_general(left, right, (((1,), (1,)), ((), ())), preferred_element_...]
    dot_general x3 -> x4, matrix products: 6.46 us -> 6.48 us  [dot_nn(): lax.dot_general(left, right, (((1,), (0,)), ((), ())), preferred_element_...]
  transfers between devices with their start and end apart: 37 -> 39, of which waited for: 24 -> 20; matrix products, arithmetic and copies ran while one was open for 19% -> 20% of each run, Pallas kernels for 0% -> 0%
where the time goes in v2:
time: 178 us
  waiting for transfers between devices  75.7 us (43%)
  starting transfers between devices  50.9 us (29%)
  matrix products  19.6 us (11%)
  other arithmetic  18.3 us (10%)
  local copies, waits for them, and re-layouts  10.6 us (6%)
  between operations  2.66 us (1%)
    ppermute x21, waiting for transfers between devices, over_gy(): return lax.ppermute(block, 'gy', GY_PAIRS[bit])  52.6 us
    ppermute x21, starting transfers between devices, over_gy(): return lax.ppermute(block, 'gy', GY_PAIRS[bit])  29.7 us
    ppermute x10, waiting for transfers between devices, over_gz(): return lax.ppermute(block, 'gz', GZ_PAIRS[step])  18.5 us
    ppermute x10, starting transfers between devices, over_gz(): return lax.ppermute(block, 'gz', GZ_PAIRS[step])  12.5 us
    ppermute x2, starting transfers between devices, over_high(): return lax.ppermute(block, 'gx', HIGH_PAIRS)  7.29 us
    dot_general x2, matrix products, dot_tn(): lax.dot_general(left, right, (((0,), (0,)), ((), ())), preferred_element_...  6.68 us
    dot_general x4, matrix products, dot_nn(): lax.dot_general(left, right, (((1,), (0,)), ((), ())), preferred_element_...  6.48 us
    dot_general x4, matrix products, dot_nt(): lax.dot_general(left, right, (((1,), (1,)), ((), ())), preferred_element_...  6.46 us
  transfers between devices with their start and end apart: 39, of which 20 were waited for; matrix products, arithmetic and copies ran while one was open for 20% of the time, Pallas kernels for 0%

profile of v2, /device:TPU:0, one launch (start us, length us, event | category | flops | bytes accessed | tf_op | source)
XLA Modules:
  0.0 177.9 jit_solution(9328481302992018181)
XLA Ops:
  2.0 3.2 %collective-permute-start.2 = (bf16[8,32,384]{2,1,0:T(8,128)(2,1)S(1)}, bf16[8,32,384]{2,1,0:T(8,128)(2,1)S(1)}, u32[]{:S(2)}, u32[]{:S(2)}) collective-permute-start(bf16[8,32,384]{2,1,0:T(8,128)(2,1)S(1)} %constant_dynamic-update-slice_fusion), channel_id=1, source_target_pairs={{0,2},{1,3},{2,0},{3,1},{4,6},{5,7},{6,4},{7,5},{8,10},{9,11},{10,... | collective-permute-start | bytes 589832 | tf_op jit(solution)/shard_map/ppermute | solution.py:59
  6.3 3.9 %collective-permute-start.4 = (bf16[8,32,384]{2,1,0:T(8,128)(2,1)S(1)}, bf16[8,32,384]{2,1,0:T(8,128)(2,1)S(1)}, u32[]{:S(2)}, u32[]{:S(2)}) collective-permute-start(bf16[8,32,384]{2,1,0:T(8,128)(2,1)S(1)} %constant_dynamic-update-slice_fusion), channel_id=1, source_target_pairs={{0,64},{32,96},{64,0},{96,32},{1,65},{33,97},{65,1},{97,33},{2,66}... | collective-permute-start | bytes 589832 | tf_op jit(solution)/shard_map/ppermute | solution.py:67
  10.5 3.8 %collective-permute-done.1 = bf16[8,32,384]{2,1,0:T(8,128)(2,1)S(1)} collective-permute-done((bf16[8,32,384]{2,1,0:T(8,128)(2,1)S(1)}, bf16[8,32,384]{2,1,0:T(8,128)(2,1)S(1)}, u32[]{:S(2)}, u32[]{:S(2)}) %collective-permute-start.1) | collective-permute-done | bytes 196640 | tf_op jit(solution)/shard_map/ppermute | solution.py:59
  24.3 5.4 %collective-permute-done.6.refs_1_ = bf16[8,32,384]{2,1,0:T(8,128)(2,1)S(1)} collective-permute-done((bf16[8,32,384]{2,1,0:T(8,128)(2,1)S(1)}, bf16[8,32,384]{2,1,0:T(8,128)(2,1)S(1)}, u32[]{:S(2)}, u32[]{:S(2)}) %collective-permute-start.6) | collective-permute-done | bytes 196640 | tf_op jit(solution)/shard_map/ppermute | solution.py:59
  38.3 2.0 %collective-permute-start.11 = (bf16[2,2,2,2,64,512]{5,4,2,1,3,0:T(8,128)(2,1)S(1)}, bf16[2,2,2,2,64,512]{5,4,2,1,3,0:T(8,128)(2,1)S(1)}, u32[]{:S(2)}, u32[]{:S(2)}) collective-permute-start(bf16[2,2,2,2,64,512]{5,4,2,1,3,0:T(8,128)(2,1)S(1)} %pad_maximum_fusion.4), channel_id=1, source_target_pairs={{0,16},{4,20},{8,24},{12,28},{16,0},{20,4},{24,8},{28,12},{1,17},{... | collective-permute-start | bytes 3145736 | tf_op jit(solution)/shard_map/ppermute | solution.py:55
  40.5 2.4 %collective-permute-start.17 = (bf16[2,2,2,2,64,512]{5,4,2,1,3,0:T(8,128)(2,1)S(1)}, bf16[2,2,2,2,64,512]{5,4,2,1,3,0:T(8,128)(2,1)S(1)}, u32[]{:S(2)}, u32[]{:S(2)}) collective-permute-start(bf16[2,2,2,2,64,512]{5,4,2,1,3,0:T(8,128)(2,1)S(1)} %pad_maximum_fusion.6), channel_id=1, source_target_pairs={{0,12},{4,8},{8,4},{12,0},{16,28},{20,24},{24,20},{28,16},{1,13},{... | collective-permute-start | bytes 3145736 | tf_op jit(solution)/shard_map/ppermute | solution.py:55
  43.3 18.4 %collective-permute-done.23 = bf16[2,2,2,2,64,512]{5,4,3,2,1,0:T(8,128)(2,1)S(1)} collective-permute-done((bf16[2,2,2,2,64,512]{5,4,3,2,1,0:T(8,128)(2,1)S(1)}, bf16[2,2,2,2,64,512]{5,4,3,2,1,0:T(8,128)(2,1)S(1)}, u32[]{:S(2)}, u32[]{:S(2)}) %collective-permute-start.23) | collective-permute-done | bytes 1048608 | tf_op jit(solution)/shard_map/ppermute | solution.py:55
  64.7 3.1 %collective-permute-start.12 = (bf16[2,2,128,512]{3,2,1,0:T(8,128)(2,1)S(1)}, bf16[2,2,128,512]{3,2,1,0:T(8,128)(2,1)S(1)}, u32[]{:S(2)}, u32[]{:S(2)}) collective-permute-start(bf16[2,2,128,512]{3,2,1,0:T(8,128)(2,1)S(1)} %slice_bitcast_fusion), channel_id=1, source_target_pairs={{0,12},{4,8},{8,4},{12,0},{16,28},{20,24},{24,20},{28,16},{1,13},{... | collective-permute-start | bytes 1572872 | tf_op jit(solution)/shard_map/ppermute | solution.py:55
  68.6 7.0 %collective-permute-done.24 = bf16[2,2,128,512]{3,2,0,1:T(8,128)(2,1)S(1)} collective-permute-done((bf16[2,2,128,512]{3,2,0,1:T(8,128)(2,1)S(1)}, bf16[2,2,128,512]{3,2,0,1:T(8,128)(2,1)S(1)}, u32[]{:S(2)}, u32[]{:S(2)}) %collective-permute-start.24) | collective-permute-done | bytes 524320 | tf_op jit(solution)/shard_map/ppermute | solution.py:55
  76.5 3.0 %collective-permute-start.25 = (bf16[2,128,512]{2,1,0:T(8,128)(2,1)}, bf16[2,128,512]{2,1,0:T(8,128)(2,1)}, u32[]{:S(2)}, u32[]{:S(2)}) collective-permute-start(bf16[2,128,512]{2,1,0:T(8,128)(2,1)} %slice_bitcast_fusion.2), channel_id=1, source_target_pairs={{0,12},{4,8},{8,4},{12,0},{16,28},{20,24},{24,20},{28,16},{1,13},{... | collective-permute-start | bytes 786440 | tf_op jit(solution)/shard_map/ppermute | solution.py:55
  83.3 3.3 %collective-permute-done.13 = bf16[2,128,512]{2,1,0:T(8,128)(2,1)S(1)} collective-permute-done((bf16[2,128,512]{2,1,0:T(8,128)(2,1)S(1)}, bf16[2,128,512]{2,1,0:T(8,128)(2,1)S(1)}, u32[]{:S(2)}, u32[]{:S(2)}) %collective-permute-start.13) | collective-permute-done | bytes 262176 | tf_op jit(solution)/shard_map/ppermute | solution.py:55
  106.9 5.7 %collective-permute-done.27 = bf16[2,2,128,512]{3,2,0,1:T(8,128)(2,1)S(1)} collective-permute-done((bf16[2,2,128,512]{3,2,0,1:T(8,128)(2,1)S(1)}, bf16[2,2,128,512]{3,2,0,1:T(8,128)(2,1)S(1)}, u32[]{:S(2)}, u32[]{:S(2)}) %collective-permute-start.27) | collective-permute-done | bytes 524320 | tf_op jit(solution)/shard_map/ppermute | solution.py:55
  112.7 2.1 %collective-permute-start.28 = (bf16[2,2,128,512]{3,2,1,0:T(8,128)(2,1)S(1)}, bf16[2,2,128,512]{3,2,1,0:T(8,128)(2,1)S(1)}, u32[]{:S(2)}, u32[]{:S(2)}) collective-permute-start(bf16[2,2,128,512]{3,2,1,0:T(8,128)(2,1)S(1)} %bitcast.362), channel_id=1, source_target_pairs={{0,4},{4,0},{8,12},{12,8},{16,20},{20,16},{24,28},{28,24},{1,5},{5... | collective-permute-start | bytes 1572872 | tf_op jit(solution)/shard_map/ppermute | solution.py:55
  115.3 3.0 %collective-permute-done.21 = bf16[2,2,128,512]{3,2,0,1:T(8,128)(2,1)S(1)} collective-permute-done((bf16[2,2,128,512]{3,2,0,1:T(8,128)(2,1)S(1)}, bf16[2,2,128,512]{3,2,0,1:T(8,128)(2,1)S(1)}, u32[]{:S(2)}, u32[]{:S(2)}) %collective-permute-start.21) | collective-permute-done | bytes 524320 | tf_op jit(solution)/shard_map/ppermute | solution.py:55
  118.4 2.4 %collective-permute-start.22 = (bf16[2,2,128,512]{3,2,1,0:T(8,128)(2,1)S(1)}, bf16[2,2,128,512]{3,2,1,0:T(8,128)(2,1)S(1)}, u32[]{:S(2)}, u32[]{:S(2)}) collective-permute-start(bf16[2,2,128,512]{3,2,1,0:T(8,128)(2,1)S(1)} %bitcast.363), channel_id=1, source_target_pairs={{0,12},{4,8},{8,4},{12,0},{16,28},{20,24},{24,20},{28,16},{1,13},{... | collective-permute-start | bytes 1572872 | tf_op jit(solution)/shard_map/ppermute | solution.py:55
  121.5 8.0 %collective-permute-done.28 = bf16[2,2,128,512]{3,2,1,0:T(8,128)(2,1)S(1)} collective-permute-done((bf16[2,2,128,512]{3,2,1,0:T(8,128)(2,1)S(1)}, bf16[2,2,128,512]{3,2,1,0:T(8,128)(2,1)S(1)}, u32[]{:S(2)}, u32[]{:S(2)}) %collective-permute-start.28) | collective-permute-done | bytes 524320 | tf_op jit(solution)/shard_map/ppermute | solution.py:55
  129.5 2.3 %collective-permute-start.31 = (bf16[2,2,128,512]{3,2,1,0:T(8,128)(2,1)S(1)}, bf16[2,2,128,512]{3,2,1,0:T(8,128)(2,1)S(1)}, u32[]{:S(2)}, u32[]{:S(2)}) collective-permute-start(bf16[2,2,128,512]{3,2,1,0:T(8,128)(2,1)S(1)} %bitcast.361), channel_id=1, source_target_pairs={{0,12},{4,8},{8,4},{12,0},{16,28},{20,24},{24,20},{28,16},{1,13},{... | collective-permute-start | bytes 1572872 | tf_op jit(solution)/shard_map/ppermute | solution.py:55
  134.7 3.6 %collective-permute-done.32 = bf16[2,2,128,512]{3,2,1,0:T(8,128)(2,1)S(1)} collective-permute-done((bf16[2,2,128,512]{3,2,1,0:T(8,128)(2,1)S(1)}, bf16[2,2,128,512]{3,2,1,0:T(8,128)(2,1)S(1)}, u32[]{:S(2)}, u32[]{:S(2)}) %collective-permute-start.32) | collective-permute-done | bytes 524320 | tf_op jit(solution)/shard_map/ppermute | solution.py:55
  148.9 2.1 %collective-permute-start.35 = (bf16[2,8,32,384]{3,2,1,0:T(8,128)(2,1)S(1)}, bf16[2,8,32,384]{3,2,1,0:T(8,128)(2,1)S(1)}, u32[]{:S(2)}, u32[]{:S(2)}) collective-permute-start(bf16[2,8,32,384]{3,2,1,0:T(8,128)(2,1)S(1)} %pad_maximum_fusion.34), channel_id=1, source_target_pairs={{0,3},{1,2},{2,1},{3,0},{4,7},{5,6},{6,5},{7,4},{8,11},{9,10},{10,... | collective-permute-start | bytes 1179656 | tf_op jit(solution)/shard_map/ppermute | solution.py:59
  151.0 3.5 %convolution_convert_fusion.1.refs_2_ = bf16[1536,768]{1,0:T(8,128)(2,1)S(1)} fusion(bf16[1024,768]{1,0:T(8,128)(2,1)S(1)} %bitcast.328, bf16[1024,512]{1,0:T(8,128)(2,1)S(1)} %bitcast.347, bf16[1024,512]{1,0:T(8,128)(2,1)S(1)} %bitcast.380, bf16[1024,512]{1,0:T(8,128)(2,1)S(1)} %bitcast.381), kind=kOutput, calls=%fused_computation.25 | convolution fusion | flops 2426535936 | bytes 7077888 | tf_op jit(solution)/shard_map/dot_general | solution.py:29
  154.6 4.8 %collective-permute-done.34.refs_0_ = bf16[2,8,32,384]{3,2,1,0:T(8,128)(2,1)S(1)} collective-permute-done((bf16[2,8,32,384]{3,2,1,0:T(8,128)(2,1)S(1)}, bf16[2,8,32,384]{3,2,1,0:T(8,128)(2,1)S(1)}, u32[]{:S(2)}, u32[]{:S(2)}) %collective-permute-start.34) | collective-permute-done | bytes 393248 | tf_op jit(solution)/shard_map/ppermute | solution.py:59
  163.0 3.2 %convolution_convert_fusion.refs_2_ = bf16[768,1536]{1,0:T(8,128)(2,1)S(1)} fusion(bf16[1024,768]{1,0:T(8,128)(2,1)S(1)} %bitcast.327, bf16[1024,512]{1,0:T(8,128)(2,1)S(1)} %bitcast.345, bf16[1024,512]{1,0:T(8,128)(2,1)S(1)} %bitcast.378, bf16[1024,512]{1,0:T(8,128)(2,1)S(1)} %bitcast.379), kind=kOutput, calls=%fused_computation.24 | convolution fusion | flops 2426535936 | bytes 7077888 | tf_op jit(solution)/shard_map/dot_general | solution.py:29
  168.7 3.4 %collective-permute-start.38 = (bf16[8,32,384]{2,1,0:T(8,128)(2,1)S(1)}, bf16[8,32,384]{2,1,0:T(8,128)(2,1)S(1)}, u32[]{:S(2)}, u32[]{:S(2)}) collective-permute-start(bf16[8,32,384]{2,1,0:T(8,128)(2,1)S(1)} %fusion.34), channel_id=1, source_target_pairs={{0,64},{32,96},{64,0},{96,32},{1,65},{33,97},{65,1},{97,33},{2,66}... | collective-permute-start | bytes 589832 | tf_op jit(solution)/shard_map/ppermute | solution.py:67
  172.1 3.8 %collective-permute-done.38 = bf16[8,32,384]{2,1,0:T(8,128)(2,1)S(1)} collective-permute-done((bf16[8,32,384]{2,1,0:T(8,128)(2,1)S(1)}, bf16[8,32,384]{2,1,0:T(8,128)(2,1)S(1)}, u32[]{:S(2)}, u32[]{:S(2)}) %collective-permute-start.38) | collective-permute-done | bytes 196640 | tf_op jit(solution)/shard_map/ppermute | solution.py:67
  (239 shorter events, 71.8 us)
Async XLA Ops:
  6.3 9.9 %collective-permute-start.4 = (bf16[8,32,384]{2,1,0:T(8,128)(2,1)S(1)}, bf16[8,32,384]{2,1,0:T(8,128)(2,1)S(1)}, u32[]{:S(2)}, u32[]{:S(2)}) collective-permute-start(bf16[8,32,384]{2,1,0:T(8,128)(2,1)S(1)} %constant_dynamic-update-slice_fusion), channel_id=1, source_target_pairs={{0,64},{32,96},{64,0},{96,32},{1,65},{33,97},{65,1},{97,33},{2,66}... | collective-permute-start | bytes 589832 | tf_op jit(solution)/shard_map/ppermute | solution.py:67
  17.7 12.1 %collective-permute-start.6 = (bf16[8,32,384]{2,1,0:T(8,128)(2,1)S(1)}, bf16[8,32,384]{2,1,0:T(8,128)(2,1)S(1)}, u32[]{:S(2)}, u32[]{:S(2)}) collective-permute-start(bf16[8,32,384]{2,1,0:T(8,128)(2,1)S(1)} %collective-permute-done.4), channel_id=1, source_target_pairs={{0,3},{1,2},{2,1},{3,0},{4,7},{5,6},{6,5},{7,4},{8,11},{9,10},{10,... | collective-permute-start | bytes 589832 | tf_op jit(solution)/shard_map/ppermute | solution.py:59
  18.9 10.9 %collective-permute-start.7 = (bf16[8,32,384]{2,1,0:T(8,128)(2,1)S(1)}, bf16[8,32,384]{2,1,0:T(8,128)(2,1)S(1)}, u32[]{:S(2)}, u32[]{:S(2)}) collective-permute-start(bf16[8,32,384]{2,1,0:T(8,128)(2,1)S(1)} %collective-permute-done.4), channel_id=1, source_target_pairs={{0,2},{1,3},{2,0},{3,1},{4,6},{5,7},{6,4},{7,5},{8,10},{9,11},{10,... | collective-permute-start | bytes 589832 | tf_op jit(solution)/shard_map/ppermute | solution.py:59
  36.4 25.3 %collective-permute-start.23 = (bf16[2,2,2,2,64,512]{5,4,3,2,1,0:T(8,128)(2,1)S(1)}, bf16[2,2,2,2,64,512]{5,4,3,2,1,0:T(8,128)(2,1)S(1)}, u32[]{:S(2)}, u32[]{:S(2)}) collective-permute-start(bf16[2,2,2,2,64,512]{5,4,3,2,1,0:T(8,128)(2,1)S(1)} %pad_maximum_fusion.8), channel_id=1, source_target_pairs={{0,4},{4,0},{8,12},{12,8},{16,20},{20,16},{24,28},{28,24},{1,5},{5... | collective-permute-start | bytes 3145736 | tf_op jit(solution)/shard_map/ppermute | solution.py:55
  38.3 25.9 %collective-permute-start.11 = (bf16[2,2,2,2,64,512]{5,4,2,1,3,0:T(8,128)(2,1)S(1)}, bf16[2,2,2,2,64,512]{5,4,2,1,3,0:T(8,128)(2,1)S(1)}, u32[]{:S(2)}, u32[]{:S(2)}) collective-permute-start(bf16[2,2,2,2,64,512]{5,4,2,1,3,0:T(8,128)(2,1)S(1)} %pad_maximum_fusion.4), channel_id=1, source_target_pairs={{0,16},{4,20},{8,24},{12,28},{16,0},{20,4},{24,8},{28,12},{1,17},{... | collective-permute-start | bytes 3145736 | tf_op jit(solution)/shard_map/ppermute | solution.py:55
  40.5 27.3 %collective-permute-start.17 = (bf16[2,2,2,2,64,512]{5,4,2,1,3,0:T(8,128)(2,1)S(1)}, bf16[2,2,2,2,64,512]{5,4,2,1,3,0:T(8,128)(2,1)S(1)}, u32[]{:S(2)}, u32[]{:S(2)}) collective-permute-start(bf16[2,2,2,2,64,512]{5,4,2,1,3,0:T(8,128)(2,1)S(1)} %pad_maximum_fusion.6), channel_id=1, source_target_pairs={{0,12},{4,8},{8,4},{12,0},{16,28},{20,24},{24,20},{28,16},{1,13},{... | collective-permute-start | bytes 3145736 | tf_op jit(solution)/shard_map/ppermute | solution.py:55
  62.2 13.4 %collective-permute-start.24 = (bf16[2,2,128,512]{3,2,0,1:T(8,128)(2,1)S(1)}, bf16[2,2,128,512]{3,2,0,1:T(8,128)(2,1)S(1)}, u32[]{:S(2)}, u32[]{:S(2)}) collective-permute-start(bf16[2,2,128,512]{3,2,0,1:T(8,128)(2,1)S(1)} %bitcast.390), channel_id=1, source_target_pairs={{0,16},{4,20},{8,24},{12,28},{16,0},{20,4},{24,8},{28,12},{1,17},{... | collective-permute-start | bytes 1572872 | tf_op jit(solution)/shard_map/ppermute | solution.py:55
  64.7 14.9 %collective-permute-start.12 = (bf16[2,2,128,512]{3,2,1,0:T(8,128)(2,1)S(1)}, bf16[2,2,128,512]{3,2,1,0:T(8,128)(2,1)S(1)}, u32[]{:S(2)}, u32[]{:S(2)}) collective-permute-start(bf16[2,2,128,512]{3,2,1,0:T(8,128)(2,1)S(1)} %slice_bitcast_fusion), channel_id=1, source_target_pairs={{0,12},{4,8},{8,4},{12,0},{16,28},{20,24},{24,20},{28,16},{1,13},{... | collective-permute-start | bytes 1572872 | tf_op jit(solution)/shard_map/ppermute | solution.py:55
  68.4 12.9 %collective-permute-start.18 = (bf16[2,2,128,512]{3,2,0,1:T(8,128)(2,1)S(1)}, bf16[2,2,128,512]{3,2,0,1:T(8,128)(2,1)S(1)}, u32[]{:S(2)}, u32[]{:S(2)}) collective-permute-start(bf16[2,2,128,512]{3,2,0,1:T(8,128)(2,1)S(1)} %bitcast.391), channel_id=1, source_target_pairs={{0,4},{4,0},{8,12},{12,8},{16,20},{20,16},{24,28},{28,24},{1,5},{5... | collective-permute-start | bytes 1572872 | tf_op jit(solution)/shard_map/ppermute | solution.py:55
  76.5 12.2 %collective-permute-start.25 = (bf16[2,128,512]{2,1,0:T(8,128)(2,1)}, bf16[2,128,512]{2,1,0:T(8,128)(2,1)}, u32[]{:S(2)}, u32[]{:S(2)}) collective-permute-start(bf16[2,128,512]{2,1,0:T(8,128)(2,1)} %slice_bitcast_fusion.2), channel_id=1, source_target_pairs={{0,12},{4,8},{8,4},{12,0},{16,28},{20,24},{24,20},{28,16},{1,13},{... | collective-permute-start | bytes 786440 | tf_op jit(solution)/shard_map/ppermute | solution.py:55
  82.9 9.7 %collective-permute-start.19 = (bf16[2,128,512]{2,1,0:T(8,128)(2,1)}, bf16[2,128,512]{2,1,0:T(8,128)(2,1)}, u32[]{:S(2)}, u32[]{:S(2)}) collective-permute-start(bf16[2,128,512]{2,1,0:T(8,128)(2,1)} %slice_bitcast_fusion.4), channel_id=1, source_target_pairs={{0,16},{4,20},{8,24},{12,28},{16,0},{20,4},{24,8},{28,12},{1,17},{... | collective-permute-start | bytes 786440 | tf_op jit(solution)/shard_map/ppermute | solution.py:55
  94.8 9.5 %collective-permute-start.20 = (bf16[2,128,512]{2,1,0:T(8,128)(2,1)}, bf16[2,128,512]{2,1,0:T(8,128)(2,1)}, u32[]{:S(2)}, u32[]{:S(2)}) collective-permute-start(bf16[2,128,512]{2,1,0:T(8,128)(2,1)} %get-tuple-element.125), channel_id=1, source_target_pairs={{0,16},{4,20},{8,24},{12,28},{16,0},{20,4},{24,8},{28,12},{1,17},{... | collective-permute-start | bytes 786440 | tf_op jit(solution)/shard_map/ppermute | solution.py:55
  100.0 12.6 %collective-permute-start.27 = (bf16[2,2,128,512]{3,2,0,1:T(8,128)(2,1)S(1)}, bf16[2,2,128,512]{3,2,0,1:T(8,128)(2,1)S(1)}, u32[]{:S(2)}, u32[]{:S(2)}) collective-permute-start(bf16[2,2,128,512]{3,2,0,1:T(8,128)(2,1)S(1)} %get-tuple-element.111), channel_id=1, source_target_pairs={{0,16},{4,20},{8,24},{12,28},{16,0},{20,4},{24,8},{28,12},{1,17},{... | collective-permute-start | bytes 1572872 | tf_op jit(solution)/shard_map/ppermute | solution.py:55
  102.8 12.0 %collective-permute-start.15 = (bf16[2,2,128,512]{3,2,0,1:T(8,128)(2,1)S(1)}, bf16[2,2,128,512]{3,2,0,1:T(8,128)(2,1)S(1)}, u32[]{:S(2)}, u32[]{:S(2)}) collective-permute-start(bf16[2,2,128,512]{3,2,0,1:T(8,128)(2,1)S(1)} %get-tuple-element.103), channel_id=1, source_target_pairs={{0,12},{4,8},{8,4},{12,0},{16,28},{20,24},{24,20},{28,16},{1,13},{... | collective-permute-start | bytes 1572872 | tf_op jit(solution)/shard_map/ppermute | solution.py:55
  105.3 13.0 %collective-permute-start.21 = (bf16[2,2,128,512]{3,2,0,1:T(8,128)(2,1)S(1)}, bf16[2,2,128,512]{3,2,0,1:T(8,128)(2,1)S(1)}, u32[]{:S(2)}, u32[]{:S(2)}) collective-permute-start(bf16[2,2,128,512]{3,2,0,1:T(8,128)(2,1)S(1)} %get-tuple-element.107), channel_id=1, source_target_pairs={{0,4},{4,0},{8,12},{12,8},{16,20},{20,16},{24,28},{28,24},{1,5},{5... | collective-permute-start | bytes 1572872 | tf_op jit(solution)/shard_map/ppermute | solution.py:55
  112.7 16.9 %collective-permute-start.28 = (bf16[2,2,128,512]{3,2,1,0:T(8,128)(2,1)S(1)}, bf16[2,2,128,512]{3,2,1,0:T(8,128)(2,1)S(1)}, u32[]{:S(2)}, u32[]{:S(2)}) collective-permute-start(bf16[2,2,128,512]{3,2,1,0:T(8,128)(2,1)S(1)} %bitcast.362), channel_id=1, source_target_pairs={{0,4},{4,0},{8,12},{12,8},{16,20},{20,16},{24,28},{28,24},{1,5},{5... | collective-permute-start | bytes 1572872 | tf_op jit(solution)/shard_map/ppermute | solution.py:55
  114.9 17.2 %collective-permute-start.16 = (bf16[2,2,128,512]{3,2,1,0:T(8,128)(2,1)S(1)}, bf16[2,2,128,512]{3,2,1,0:T(8,128)(2,1)S(1)}, u32[]{:S(2)}, u32[]{:S(2)}) collective-permute-start(bf16[2,2,128,512]{3,2,1,0:T(8,128)(2,1)S(1)} %bitcast.335), channel_id=1, source_target_pairs={{0,16},{4,20},{8,24},{12,28},{16,0},{20,4},{24,8},{28,12},{1,17},{... | collective-permute-start | bytes 1572872 | tf_op jit(solution)/shard_map/ppermute | solution.py:55
  118.4 13.5 %collective-permute-start.22 = (bf16[2,2,128,512]{3,2,1,0:T(8,128)(2,1)S(1)}, bf16[2,2,128,512]{3,2,1,0:T(8,128)(2,1)S(1)}, u32[]{:S(2)}, u32[]{:S(2)}) collective-permute-start(bf16[2,2,128,512]{3,2,1,0:T(8,128)(2,1)S(1)} %bitcast.363), channel_id=1, source_target_pairs={{0,12},{4,8},{8,4},{12,0},{16,28},{20,24},{24,20},{28,16},{1,13},{... | collective-permute-start | bytes 1572872 | tf_op jit(solution)/shard_map/ppermute | solution.py:55
  121.0 17.3 %collective-permute-start.32 = (bf16[2,2,128,512]{3,2,1,0:T(8,128)(2,1)S(1)}, bf16[2,2,128,512]{3,2,1,0:T(8,128)(2,1)S(1)}, u32[]{:S(2)}, u32[]{:S(2)}) collective-permute-start(bf16[2,2,128,512]{3,2,1,0:T(8,128)(2,1)S(1)} %bitcast.360), channel_id=1, source_target_pairs={{0,4},{4,0},{8,12},{12,8},{16,20},{20,16},{24,28},{28,24},{1,5},{5... | collective-permute-start | bytes 1572872 | tf_op jit(solution)/shard_map/ppermute | solution.py:55
  121.1 19.1 %collective-permute-start.30 = (bf16[2,2,128,512]{3,2,1,0:T(8,128)(2,1)S(1)}, bf16[2,2,128,512]{3,2,1,0:T(8,128)(2,1)S(1)}, u32[]{:S(2)}, u32[]{:S(2)}) collective-permute-start(bf16[2,2,128,512]{3,2,1,0:T(8,128)(2,1)S(1)} %bitcast.332), channel_id=1, source_target_pairs={{0,16},{4,20},{8,24},{12,28},{16,0},{20,4},{24,8},{28,12},{1,17},{... | collective-permute-start | bytes 1572872 | tf_op jit(solution)/shard_map/ppermute | solution.py:55
  129.5 10.6 %collective-permute-start.31 = (bf16[2,2,128,512]{3,2,1,0:T(8,128)(2,1)S(1)}, bf16[2,2,128,512]{3,2,1,0:T(8,128)(2,1)S(1)}, u32[]{:S(2)}, u32[]{:S(2)}) collective-permute-start(bf16[2,2,128,512]{3,2,1,0:T(8,128)(2,1)S(1)} %bitcast.361), channel_id=1, source_target_pairs={{0,12},{4,8},{8,4},{12,0},{16,28},{20,24},{24,20},{28,16},{1,13},{... | collective-permute-start | bytes 1572872 | tf_op jit(solution)/shard_map/ppermute | solution.py:55
  134.6 9.8 %collective-permute-start.29 = (bf16[512,1024]{1,0:T(8,128)(2,1)S(1)}, bf16[512,1024]{1,0:T(8,128)(2,1)S(1)}, u32[]{:S(2)}, u32[]{:S(2)}) collective-permute-start(bf16[512,1024]{1,0:T(8,128)(2,1)S(1)} %convolution_convert_fusion.7), channel_id=1, source_target_pairs={{0,32},{32,0},{64,96},{96,64},{1,33},{33,1},{65,97},{97,65},{2,34}... | collective-permute-start | bytes 3145736 | tf_op jit(solution)/shard_map/ppermute | solution.py:63
  148.7 10.7 %collective-permute-start.34 = (bf16[2,8,32,384]{3,2,1,0:T(8,128)(2,1)S(1)}, bf16[2,8,32,384]{3,2,1,0:T(8,128)(2,1)S(1)}, u32[]{:S(2)}, u32[]{:S(2)}) collective-permute-start(bf16[2,8,32,384]{3,2,1,0:T(8,128)(2,1)S(1)} %pad_maximum_fusion.33), channel_id=1, source_target_pairs={{0,1},{1,0},{2,3},{3,2},{4,5},{5,4},{6,7},{7,6},{8,9},{9,8},{10,11... | collective-permute-start | bytes 1179656 | tf_op jit(solution)/shard_map/ppermute | solution.py:59
  148.9 11.9 %collective-permute-start.35 = (bf16[2,8,32,384]{3,2,1,0:T(8,128)(2,1)S(1)}, bf16[2,8,32,384]{3,2,1,0:T(8,128)(2,1)S(1)}, u32[]{:S(2)}, u32[]{:S(2)}) collective-permute-start(bf16[2,8,32,384]{3,2,1,0:T(8,128)(2,1)S(1)} %pad_maximum_fusion.34), channel_id=1, source_target_pairs={{0,3},{1,2},{2,1},{3,0},{4,7},{5,6},{6,5},{7,4},{8,11},{9,10},{10,... | collective-permute-start | bytes 1179656 | tf_op jit(solution)/shard_map/ppermute | solution.py:59
  (30 other events, 146.7 us)

commit v3 on v2

--- a/solution.py
+++ b/solution.py
@@ -47,7 +47,7 @@
 HIGH_PAIRS = [(g, g ^ 2) for g in range(4)]
 
 PARTS = 3
-ORDERS = ((2, 1, 0), (1, 0, 2), (0, 2, 1))
+ORDERS = ((1, 0, 2), (0, 2, 1), (2, 1, 0))
 SLOT = 256
 
 

time: 178 us -> 179 us (level)
  waiting for transfers between devices: 75.7 us -> 82.7 us
  starting transfers between devices: 50.9 us -> 47.4 us
  other arithmetic: 18.3 us -> 15.2 us
    ppermute x21, waiting for transfers between devices: 52.6 us -> 59.8 us  [over_gy(): return lax.ppermute(block, 'gy', GY_PAIRS[bit])]
    ppermute x21, starting transfers between devices: 29.7 us -> 25.6 us  [over_gy(): return lax.ppermute(block, 'gy', GY_PAIRS[bit])]
    another operation x6, other arithmetic: 3.33 us -> 1.43 us  [per_device(): square = jnp.stack([pair, over_gy(pair, second)], axis=1)]
    unnamed x48 -> x54, local copies, waits for them, and re-layouts: 5.39 us -> 6.28 us
  transfers between devices with their start and end apart: 39 -> 39, of which waited for: 20 -> 21; matrix products, arithmetic and copies ran while one was open for 20% -> 19% of each run, Pallas kernels for 0% -> 0%
where the time goes in v3:
time: 179 us
  waiting for transfers between devices  82.7 us (46%)
  starting transfers between devices  47.4 us (26%)
  matrix products  19.6 us (11%)
  other arithmetic  15.2 us (8%)
  local copies, waits for them, and re-layouts  11.5 us (6%)
  between operations  2.72 us (2%)
    ppermute x21, waiting for transfers between devices, over_gy(): return lax.ppermute(block, 'gy', GY_PAIRS[bit])  59.8 us
    ppermute x21, starting transfers between devices, over_gy(): return lax.ppermute(block, 'gy', GY_PAIRS[bit])  25.6 us
    ppermute x10, waiting for transfers between devices, over_gz(): return lax.ppermute(block, 'gz', GZ_PAIRS[step])  18.5 us
    ppermute x10, starting transfers between devices, over_gz(): return lax.ppermute(block, 'gz', GZ_PAIRS[step])  12.5 us
    ppermute x2, starting transfers between devices, over_high(): return lax.ppermute(block, 'gx', HIGH_PAIRS)  7.79 us
    dot_general x2, matrix products, dot_tn(): lax.dot_general(left, right, (((0,), (0,)), ((), ())), preferred_element_...  6.68 us
    dot_general x4, matrix products, dot_nn(): lax.dot_general(left, right, (((1,), (0,)), ((), ())), preferred_element_...  6.48 us
    dot_general x4, matrix products, dot_nt(): lax.dot_general(left, right, (((1,), (1,)), ((), ())), preferred_element_...  6.47 us
  transfers between devices with their start and end apart: 39, of which 21 were waited for; matrix products, arithmetic and copies ran while one was open for 19% of the time, Pallas kernels for 0%

profile of v3, /device:TPU:0, one launch (start us, length us, event | category | flops | bytes accessed | tf_op | source)
XLA Modules:
  0.0 179.1 jit_solution(11105214769605247934)
XLA Ops:
  2.0 3.2 %collective-permute-start.2 = (bf16[8,32,384]{2,1,0:T(8,128)(2,1)S(1)}, bf16[8,32,384]{2,1,0:T(8,128)(2,1)S(1)}, u32[]{:S(2)}, u32[]{:S(2)}) collective-permute-start(bf16[8,32,384]{2,1,0:T(8,128)(2,1)S(1)} %constant_dynamic-update-slice_fusion), channel_id=1, source_target_pairs={{0,2},{1,3},{2,0},{3,1},{4,6},{5,7},{6,4},{7,5},{8,10},{9,11},{10,... | collective-permute-start | bytes 589832 | tf_op jit(solution)/shard_map/ppermute | solution.py:59
  6.3 3.9 %collective-permute-start.4 = (bf16[8,32,384]{2,1,0:T(8,128)(2,1)S(1)}, bf16[8,32,384]{2,1,0:T(8,128)(2,1)S(1)}, u32[]{:S(2)}, u32[]{:S(2)}) collective-permute-start(bf16[8,32,384]{2,1,0:T(8,128)(2,1)S(1)} %constant_dynamic-update-slice_fusion), channel_id=1, source_target_pairs={{0,64},{32,96},{64,0},{96,32},{1,65},{33,97},{65,1},{97,33},{2,66}... | collective-permute-start | bytes 589832 | tf_op jit(solution)/shard_map/ppermute | solution.py:67
  10.5 3.8 %collective-permute-done.1 = bf16[8,32,384]{2,1,0:T(8,128)(2,1)S(1)} collective-permute-done((bf16[8,32,384]{2,1,0:T(8,128)(2,1)S(1)}, bf16[8,32,384]{2,1,0:T(8,128)(2,1)S(1)}, u32[]{:S(2)}, u32[]{:S(2)}) %collective-permute-start.1) | collective-permute-done | bytes 196640 | tf_op jit(solution)/shard_map/ppermute | solution.py:59
  24.3 5.4 %collective-permute-done.6.refs_1_ = bf16[8,32,384]{2,1,0:T(8,128)(2,1)S(1)} collective-permute-done((bf16[8,32,384]{2,1,0:T(8,128)(2,1)S(1)}, bf16[8,32,384]{2,1,0:T(8,128)(2,1)S(1)}, u32[]{:S(2)}, u32[]{:S(2)}) %collective-permute-start.6) | collective-permute-done | bytes 196640 | tf_op jit(solution)/shard_map/ppermute | solution.py:59
  36.4 3.1 %collective-permute-start.11 = (bf16[2,2,2,2,64,512]{5,4,2,1,3,0:T(8,128)(2,1)S(1)}, bf16[2,2,2,2,64,512]{5,4,2,1,3,0:T(8,128)(2,1)S(1)}, u32[]{:S(2)}, u32[]{:S(2)}) collective-permute-start(bf16[2,2,2,2,64,512]{5,4,2,1,3,0:T(8,128)(2,1)S(1)} %pad_maximum_fusion.2), channel_id=1, source_target_pairs={{0,12},{4,8},{8,4},{12,0},{16,28},{20,24},{24,20},{28,16},{1,13},{... | collective-permute-start | bytes 3145736 | tf_op jit(solution)/shard_map/ppermute | solution.py:55
  40.2 2.2 %collective-permute-start.23 = (bf16[2,2,2,2,64,512]{5,4,2,1,3,0:T(8,128)(2,1)S(1)}, bf16[2,2,2,2,64,512]{5,4,2,1,3,0:T(8,128)(2,1)S(1)}, u32[]{:S(2)}, u32[]{:S(2)}) collective-permute-start(bf16[2,2,2,2,64,512]{5,4,2,1,3,0:T(8,128)(2,1)S(1)} %pad_maximum_fusion.6), channel_id=1, source_target_pairs={{0,16},{4,20},{8,24},{12,28},{16,0},{20,4},{24,8},{28,12},{1,17},{... | collective-permute-start | bytes 3145736 | tf_op jit(solution)/shard_map/ppermute | solution.py:55
  42.7 20.3 %collective-permute-done.11 = bf16[2,2,2,2,64,512]{5,4,2,1,3,0:T(8,128)(2,1)S(1)} collective-permute-done((bf16[2,2,2,2,64,512]{5,4,2,1,3,0:T(8,128)(2,1)S(1)}, bf16[2,2,2,2,64,512]{5,4,2,1,3,0:T(8,128)(2,1)S(1)}, u32[]{:S(2)}, u32[]{:S(2)}) %collective-permute-start.11) | collective-permute-done | bytes 1048608 | tf_op jit(solution)/shard_map/ppermute | solution.py:55
  69.6 7.1 %collective-permute-done.12 = bf16[2,2,128,512]{3,2,1,0:T(8,128)(2,1)S(1)} collective-permute-done((bf16[2,2,128,512]{3,2,1,0:T(8,128)(2,1)S(1)}, bf16[2,2,128,512]{3,2,1,0:T(8,128)(2,1)S(1)}, u32[]{:S(2)}, u32[]{:S(2)}) %collective-permute-start.12) | collective-permute-done | bytes 524320 | tf_op jit(solution)/shard_map/ppermute | solution.py:55
  79.8 2.9 %collective-permute-start.19 = (bf16[2,128,512]{2,1,0:T(8,128)(2,1)}, bf16[2,128,512]{2,1,0:T(8,128)(2,1)}, u32[]{:S(2)}, u32[]{:S(2)}) collective-permute-start(bf16[2,128,512]{2,1,0:T(8,128)(2,1)} %slice_bitcast_fusion.12), channel_id=1, source_target_pairs={{0,12},{4,8},{8,4},{12,0},{16,28},{20,24},{24,20},{28,16},{1,13},{... | collective-permute-start | bytes 786440 | tf_op jit(solution)/shard_map/ppermute | solution.py:55
  89.9 2.9 %collective-permute-start.20 = (bf16[2,128,512]{2,1,0:T(8,128)(2,1)}, bf16[2,128,512]{2,1,0:T(8,128)(2,1)}, u32[]{:S(2)}, u32[]{:S(2)}) collective-permute-start(bf16[2,128,512]{2,1,0:T(8,128)(2,1)} %get-tuple-element.129), channel_id=1, source_target_pairs={{0,12},{4,8},{8,4},{12,0},{16,28},{20,24},{24,20},{28,16},{1,13},{... | collective-permute-start | bytes 786440 | tf_op jit(solution)/shard_map/ppermute | solution.py:55
  98.5 4.9 %collective-permute-done.14 = bf16[2,128,512]{2,1,0:T(8,128)(2,1)S(1)} collective-permute-done((bf16[2,128,512]{2,1,0:T(8,128)(2,1)S(1)}, bf16[2,128,512]{2,1,0:T(8,128)(2,1)S(1)}, u32[]{:S(2)}, u32[]{:S(2)}) %collective-permute-start.14) | collective-permute-done | bytes 262176 | tf_op jit(solution)/shard_map/ppermute | solution.py:55
  105.0 2.6 %collective-permute-done.26 = bf16[2,128,512]{2,1,0:T(8,128)(2,1)S(1)} collective-permute-done((bf16[2,128,512]{2,1,0:T(8,128)(2,1)S(1)}, bf16[2,128,512]{2,1,0:T(8,128)(2,1)S(1)}, u32[]{:S(2)}, u32[]{:S(2)}) %collective-permute-start.26) | collective-permute-done | bytes 262176 | tf_op jit(solution)/shard_map/ppermute | solution.py:55
  108.6 6.6 %collective-permute-done.15 = bf16[2,2,128,512]{3,2,0,1:T(8,128)(2,1)S(1)} collective-permute-done((bf16[2,2,128,512]{3,2,0,1:T(8,128)(2,1)S(1)}, bf16[2,2,128,512]{3,2,0,1:T(8,128)(2,1)S(1)}, u32[]{:S(2)}, u32[]{:S(2)}) %collective-permute-start.15) | collective-permute-done | bytes 524320 | tf_op jit(solution)/shard_map/ppermute | solution.py:55
  116.7 3.6 %collective-permute-done.27 = bf16[2,2,128,512]{3,2,0,1:T(8,128)(2,1)S(1)} collective-permute-done((bf16[2,2,128,512]{3,2,0,1:T(8,128)(2,1)S(1)}, bf16[2,2,128,512]{3,2,0,1:T(8,128)(2,1)S(1)}, u32[]{:S(2)}, u32[]{:S(2)}) %collective-permute-start.27) | collective-permute-done | bytes 524320 | tf_op jit(solution)/shard_map/ppermute | solution.py:55
  120.4 2.6 %collective-permute-start.28 = (bf16[2,2,128,512]{3,2,1,0:T(8,128)(2,1)S(1)}, bf16[2,2,128,512]{3,2,1,0:T(8,128)(2,1)S(1)}, u32[]{:S(2)}, u32[]{:S(2)}) collective-permute-start(bf16[2,2,128,512]{3,2,1,0:T(8,128)(2,1)S(1)} %bitcast.335), channel_id=1, source_target_pairs={{0,16},{4,20},{8,24},{12,28},{16,0},{20,4},{24,8},{28,12},{1,17},{... | collective-permute-start | bytes 1572872 | tf_op jit(solution)/shard_map/ppermute | solution.py:55
  123.0 8.6 %collective-permute-done.16 = bf16[2,2,128,512]{3,2,1,0:T(8,128)(2,1)S(1)} collective-permute-done((bf16[2,2,128,512]{3,2,1,0:T(8,128)(2,1)S(1)}, bf16[2,2,128,512]{3,2,1,0:T(8,128)(2,1)S(1)}, u32[]{:S(2)}, u32[]{:S(2)}) %collective-permute-start.16) | collective-permute-done | bytes 524320 | tf_op jit(solution)/shard_map/ppermute | solution.py:55
  131.6 2.5 %collective-permute-start.32 = (bf16[2,2,128,512]{3,2,1,0:T(8,128)(2,1)S(1)}, bf16[2,2,128,512]{3,2,1,0:T(8,128)(2,1)S(1)}, u32[]{:S(2)}, u32[]{:S(2)}) collective-permute-start(bf16[2,2,128,512]{3,2,1,0:T(8,128)(2,1)S(1)} %bitcast.332), channel_id=1, source_target_pairs={{0,16},{4,20},{8,24},{12,28},{16,0},{20,4},{24,8},{28,12},{1,17},{... | collective-permute-start | bytes 1572872 | tf_op jit(solution)/shard_map/ppermute | solution.py:55
  136.9 3.7 %collective-permute-done.30 = bf16[2,2,128,512]{3,2,1,0:T(8,128)(2,1)S(1)} collective-permute-done((bf16[2,2,128,512]{3,2,1,0:T(8,128)(2,1)S(1)}, bf16[2,2,128,512]{3,2,1,0:T(8,128)(2,1)S(1)}, u32[]{:S(2)}, u32[]{:S(2)}) %collective-permute-start.30) | collective-permute-done | bytes 524320 | tf_op jit(solution)/shard_map/ppermute | solution.py:55
  149.8 2.1 %collective-permute-start.35 = (bf16[2,8,32,384]{3,2,1,0:T(8,128)(2,1)S(1)}, bf16[2,8,32,384]{3,2,1,0:T(8,128)(2,1)S(1)}, u32[]{:S(2)}, u32[]{:S(2)}) collective-permute-start(bf16[2,8,32,384]{3,2,1,0:T(8,128)(2,1)S(1)} %pad_maximum_fusion.32), channel_id=1, source_target_pairs={{0,3},{1,2},{2,1},{3,0},{4,7},{5,6},{6,5},{7,4},{8,11},{9,10},{10,... | collective-permute-start | bytes 1179656 | tf_op jit(solution)/shard_map/ppermute | solution.py:59
  151.9 3.5 %convolution_convert_fusion.1.refs_2_ = bf16[1536,768]{1,0:T(8,128)(2,1)S(1)} fusion(bf16[1024,768]{1,0:T(8,128)(2,1)S(1)} %bitcast.328, bf16[1024,512]{1,0:T(8,128)(2,1)S(1)} %bitcast.381, bf16[1024,512]{1,0:T(8,128)(2,1)S(1)} %bitcast.346, bf16[1024,512]{1,0:T(8,128)(2,1)S(1)} %bitcast.380), kind=kOutput, calls=%fused_computation.25 | convolution fusion | flops 2426535936 | bytes 7077888 | tf_op jit(solution)/shard_map/dot_general | solution.py:29
  155.5 4.8 %collective-permute-done.34.refs_0_ = bf16[2,8,32,384]{3,2,1,0:T(8,128)(2,1)S(1)} collective-permute-done((bf16[2,8,32,384]{3,2,1,0:T(8,128)(2,1)S(1)}, bf16[2,8,32,384]{3,2,1,0:T(8,128)(2,1)S(1)}, u32[]{:S(2)}, u32[]{:S(2)}) %collective-permute-start.34) | collective-permute-done | bytes 393248 | tf_op jit(solution)/shard_map/ppermute | solution.py:59
  163.9 3.2 %convolution_convert_fusion.refs_2_ = bf16[768,1536]{1,0:T(8,128)(2,1)S(1)} fusion(bf16[1024,768]{1,0:T(8,128)(2,1)S(1)} %bitcast.327, bf16[1024,512]{1,0:T(8,128)(2,1)S(1)} %bitcast.379, bf16[1024,512]{1,0:T(8,128)(2,1)S(1)} %bitcast.344, bf16[1024,512]{1,0:T(8,128)(2,1)S(1)} %bitcast.378), kind=kOutput, calls=%fused_computation.24 | convolution fusion | flops 2426535936 | bytes 7077888 | tf_op jit(solution)/shard_map/dot_general | solution.py:29
  169.6 3.9 %collective-permute-start.38 = (bf16[8,32,384]{2,1,0:T(8,128)(2,1)S(1)}, bf16[8,32,384]{2,1,0:T(8,128)(2,1)S(1)}, u32[]{:S(2)}, u32[]{:S(2)}) collective-permute-start(bf16[8,32,384]{2,1,0:T(8,128)(2,1)S(1)} %fusion.34), channel_id=1, source_target_pairs={{0,64},{32,96},{64,0},{96,32},{1,65},{33,97},{65,1},{97,33},{2,66}... | collective-permute-start | bytes 589832 | tf_op jit(solution)/shard_map/ppermute | solution.py:67
  173.5 3.6 %collective-permute-done.38 = bf16[8,32,384]{2,1,0:T(8,128)(2,1)S(1)} collective-permute-done((bf16[8,32,384]{2,1,0:T(8,128)(2,1)S(1)}, bf16[8,32,384]{2,1,0:T(8,128)(2,1)S(1)}, u32[]{:S(2)}, u32[]{:S(2)}) %collective-permute-start.38) | collective-permute-done | bytes 196640 | tf_op jit(solution)/shard_map/ppermute | solution.py:67
  (245 shorter events, 65.5 us)
Async XLA Ops:
  5.2 9.1 %collective-permute-start.1 = (bf16[8,32,384]{2,1,0:T(8,128)(2,1)S(1)}, bf16[8,32,384]{2,1,0:T(8,128)(2,1)S(1)}, u32[]{:S(2)}, u32[]{:S(2)}) collective-permute-start(bf16[8,32,384]{2,1,0:T(8,128)(2,1)S(1)} %constant_dynamic-update-slice_fusion), channel_id=1, source_target_pairs={{0,3},{1,2},{2,1},{3,0},{4,7},{5,6},{6,5},{7,4},{8,11},{9,10},{10,... | collective-permute-start | bytes 589832 | tf_op jit(solution)/shard_map/ppermute | solution.py:59
  6.3 9.9 %collective-permute-start.4 = (bf16[8,32,384]{2,1,0:T(8,128)(2,1)S(1)}, bf16[8,32,384]{2,1,0:T(8,128)(2,1)S(1)}, u32[]{:S(2)}, u32[]{:S(2)}) collective-permute-start(bf16[8,32,384]{2,1,0:T(8,128)(2,1)S(1)} %constant_dynamic-update-slice_fusion), channel_id=1, source_target_pairs={{0,64},{32,96},{64,0},{96,32},{1,65},{33,97},{65,1},{97,33},{2,66}... | collective-permute-start | bytes 589832 | tf_op jit(solution)/shard_map/ppermute | solution.py:67
  17.7 12.1 %collective-permute-start.6 = (bf16[8,32,384]{2,1,0:T(8,128)(2,1)S(1)}, bf16[8,32,384]{2,1,0:T(8,128)(2,1)S(1)}, u32[]{:S(2)}, u32[]{:S(2)}) collective-permute-start(bf16[8,32,384]{2,1,0:T(8,128)(2,1)S(1)} %collective-permute-done.4), channel_id=1, source_target_pairs={{0,3},{1,2},{2,1},{3,0},{4,7},{5,6},{6,5},{7,4},{8,11},{9,10},{10,... | collective-permute-start | bytes 589832 | tf_op jit(solution)/shard_map/ppermute | solution.py:59
  18.9 10.9 %collective-permute-start.7 = (bf16[8,32,384]{2,1,0:T(8,128)(2,1)S(1)}, bf16[8,32,384]{2,1,0:T(8,128)(2,1)S(1)}, u32[]{:S(2)}, u32[]{:S(2)}) collective-permute-start(bf16[8,32,384]{2,1,0:T(8,128)(2,1)S(1)} %collective-permute-done.4), channel_id=1, source_target_pairs={{0,2},{1,3},{2,0},{3,1},{4,6},{5,7},{6,4},{7,5},{8,10},{9,11},{10,... | collective-permute-start | bytes 589832 | tf_op jit(solution)/shard_map/ppermute | solution.py:59
  36.4 26.6 %collective-permute-start.11 = (bf16[2,2,2,2,64,512]{5,4,2,1,3,0:T(8,128)(2,1)S(1)}, bf16[2,2,2,2,64,512]{5,4,2,1,3,0:T(8,128)(2,1)S(1)}, u32[]{:S(2)}, u32[]{:S(2)}) collective-permute-start(bf16[2,2,2,2,64,512]{5,4,2,1,3,0:T(8,128)(2,1)S(1)} %pad_maximum_fusion.2), channel_id=1, source_target_pairs={{0,12},{4,8},{8,4},{12,0},{16,28},{20,24},{24,20},{28,16},{1,13},{... | collective-permute-start | bytes 3145736 | tf_op jit(solution)/shard_map/ppermute | solution.py:55
  39.7 25.0 %collective-permute-start.17 = (bf16[2,2,2,2,64,512]{5,4,3,2,1,0:T(8,128)(2,1)S(1)}, bf16[2,2,2,2,64,512]{5,4,3,2,1,0:T(8,128)(2,1)S(1)}, u32[]{:S(2)}, u32[]{:S(2)}) collective-permute-start(bf16[2,2,2,2,64,512]{5,4,3,2,1,0:T(8,128)(2,1)S(1)} %pad_maximum_fusion.4), channel_id=1, source_target_pairs={{0,4},{4,0},{8,12},{12,8},{16,20},{20,16},{24,28},{28,24},{1,5},{5... | collective-permute-start | bytes 3145736 | tf_op jit(solution)/shard_map/ppermute | solution.py:55
  40.2 27.0 %collective-permute-start.23 = (bf16[2,2,2,2,64,512]{5,4,2,1,3,0:T(8,128)(2,1)S(1)}, bf16[2,2,2,2,64,512]{5,4,2,1,3,0:T(8,128)(2,1)S(1)}, u32[]{:S(2)}, u32[]{:S(2)}) collective-permute-start(bf16[2,2,2,2,64,512]{5,4,2,1,3,0:T(8,128)(2,1)S(1)} %pad_maximum_fusion.6), channel_id=1, source_target_pairs={{0,16},{4,20},{8,24},{12,28},{16,0},{20,4},{24,8},{28,12},{1,17},{... | collective-permute-start | bytes 3145736 | tf_op jit(solution)/shard_map/ppermute | solution.py:55
  63.4 13.3 %collective-permute-start.12 = (bf16[2,2,128,512]{3,2,1,0:T(8,128)(2,1)S(1)}, bf16[2,2,128,512]{3,2,1,0:T(8,128)(2,1)S(1)}, u32[]{:S(2)}, u32[]{:S(2)}) collective-permute-start(bf16[2,2,128,512]{3,2,1,0:T(8,128)(2,1)S(1)} %slice_bitcast_fusion), channel_id=1, source_target_pairs={{0,4},{4,0},{8,12},{12,8},{16,20},{20,16},{24,28},{28,24},{1,5},{5... | collective-permute-start | bytes 1572872 | tf_op jit(solution)/shard_map/ppermute | solution.py:55
  65.2 13.7 %collective-permute-start.18 = (bf16[2,2,128,512]{3,2,0,1:T(8,128)(2,1)S(1)}, bf16[2,2,128,512]{3,2,0,1:T(8,128)(2,1)S(1)}, u32[]{:S(2)}, u32[]{:S(2)}) collective-permute-start(bf16[2,2,128,512]{3,2,0,1:T(8,128)(2,1)S(1)} %bitcast.390), channel_id=1, source_target_pairs={{0,16},{4,20},{8,24},{12,28},{16,0},{20,4},{24,8},{28,12},{1,17},{... | collective-permute-start | bytes 1572872 | tf_op jit(solution)/shard_map/ppermute | solution.py:55
  67.7 15.0 %collective-permute-start.24 = (bf16[2,2,128,512]{3,2,0,1:T(8,128)(2,1)S(1)}, bf16[2,2,128,512]{3,2,0,1:T(8,128)(2,1)S(1)}, u32[]{:S(2)}, u32[]{:S(2)}) collective-permute-start(bf16[2,2,128,512]{3,2,0,1:T(8,128)(2,1)S(1)} %bitcast.391), channel_id=1, source_target_pairs={{0,12},{4,8},{8,4},{12,0},{16,28},{20,24},{24,20},{28,16},{1,13},{... | collective-permute-start | bytes 1572872 | tf_op jit(solution)/shard_map/ppermute | solution.py:55
  84.4 12.7 %collective-permute-start.25 = (bf16[2,128,512]{2,1,0:T(8,128)(2,1)}, bf16[2,128,512]{2,1,0:T(8,128)(2,1)}, u32[]{:S(2)}, u32[]{:S(2)}) collective-permute-start(bf16[2,128,512]{2,1,0:T(8,128)(2,1)} %slice_bitcast_fusion.2), channel_id=1, source_target_pairs={{0,4},{4,0},{8,12},{12,8},{16,20},{20,16},{24,28},{28,24},{1,5},{5... | collective-permute-start | bytes 786440 | tf_op jit(solution)/shard_map/ppermute | solution.py:55
  89.9 13.8 %collective-permute-start.20 = (bf16[2,128,512]{2,1,0:T(8,128)(2,1)}, bf16[2,128,512]{2,1,0:T(8,128)(2,1)}, u32[]{:S(2)}, u32[]{:S(2)}) collective-permute-start(bf16[2,128,512]{2,1,0:T(8,128)(2,1)} %get-tuple-element.129), channel_id=1, source_target_pairs={{0,12},{4,8},{8,4},{12,0},{16,28},{20,24},{24,20},{28,16},{1,13},{... | collective-permute-start | bytes 786440 | tf_op jit(solution)/shard_map/ppermute | solution.py:55
  98.3 9.2 %collective-permute-start.26 = (bf16[2,128,512]{2,1,0:T(8,128)(2,1)S(1)}, bf16[2,128,512]{2,1,0:T(8,128)(2,1)S(1)}, u32[]{:S(2)}, u32[]{:S(2)}) collective-permute-start(bf16[2,128,512]{2,1,0:T(8,128)(2,1)S(1)} %get-tuple-element.127), channel_id=1, source_target_pairs={{0,4},{4,0},{8,12},{12,8},{16,20},{20,16},{24,28},{28,24},{1,5},{5... | collective-permute-start | bytes 786440 | tf_op jit(solution)/shard_map/ppermute | solution.py:55
  103.5 11.7 %collective-permute-start.15 = (bf16[2,2,128,512]{3,2,0,1:T(8,128)(2,1)S(1)}, bf16[2,2,128,512]{3,2,0,1:T(8,128)(2,1)S(1)}, u32[]{:S(2)}, u32[]{:S(2)}) collective-permute-start(bf16[2,2,128,512]{3,2,0,1:T(8,128)(2,1)S(1)} %get-tuple-element.115), channel_id=1, source_target_pairs={{0,4},{4,0},{8,12},{12,8},{16,20},{20,16},{24,28},{28,24},{1,5},{5... | collective-permute-start | bytes 1572872 | tf_op jit(solution)/shard_map/ppermute | solution.py:55
  104.7 11.6 %collective-permute-start.21 = (bf16[2,2,128,512]{3,2,0,1:T(8,128)(2,1)S(1)}, bf16[2,2,128,512]{3,2,0,1:T(8,128)(2,1)S(1)}, u32[]{:S(2)}, u32[]{:S(2)}) collective-permute-start(bf16[2,2,128,512]{3,2,0,1:T(8,128)(2,1)S(1)} %get-tuple-element.111), channel_id=1, source_target_pairs={{0,16},{4,20},{8,24},{12,28},{16,0},{20,4},{24,8},{28,12},{1,17},{... | collective-permute-start | bytes 1572872 | tf_op jit(solution)/shard_map/ppermute | solution.py:55
  107.6 12.7 %collective-permute-start.27 = (bf16[2,2,128,512]{3,2,0,1:T(8,128)(2,1)S(1)}, bf16[2,2,128,512]{3,2,0,1:T(8,128)(2,1)S(1)}, u32[]{:S(2)}, u32[]{:S(2)}) collective-permute-start(bf16[2,2,128,512]{3,2,0,1:T(8,128)(2,1)S(1)} %get-tuple-element.107), channel_id=1, source_target_pairs={{0,12},{4,8},{8,4},{12,0},{16,28},{20,24},{24,20},{28,16},{1,13},{... | collective-permute-start | bytes 1572872 | tf_op jit(solution)/shard_map/ppermute | solution.py:55
  115.4 16.2 %collective-permute-start.16 = (bf16[2,2,128,512]{3,2,1,0:T(8,128)(2,1)S(1)}, bf16[2,2,128,512]{3,2,1,0:T(8,128)(2,1)S(1)}, u32[]{:S(2)}, u32[]{:S(2)}) collective-permute-start(bf16[2,2,128,512]{3,2,1,0:T(8,128)(2,1)S(1)} %bitcast.362), channel_id=1, source_target_pairs={{0,12},{4,8},{8,4},{12,0},{16,28},{20,24},{24,20},{28,16},{1,13},{... | collective-permute-start | bytes 1572872 | tf_op jit(solution)/shard_map/ppermute | solution.py:55
  116.4 17.8 %collective-permute-start.22 = (bf16[2,2,128,512]{3,2,1,0:T(8,128)(2,1)S(1)}, bf16[2,2,128,512]{3,2,1,0:T(8,128)(2,1)S(1)}, u32[]{:S(2)}, u32[]{:S(2)}) collective-permute-start(bf16[2,2,128,512]{3,2,1,0:T(8,128)(2,1)S(1)} %bitcast.363), channel_id=1, source_target_pairs={{0,4},{4,0},{8,12},{12,8},{16,20},{20,16},{24,28},{28,24},{1,5},{5... | collective-permute-start | bytes 1572872 | tf_op jit(solution)/shard_map/ppermute | solution.py:55
  120.4 14.1 %collective-permute-start.28 = (bf16[2,2,128,512]{3,2,1,0:T(8,128)(2,1)S(1)}, bf16[2,2,128,512]{3,2,1,0:T(8,128)(2,1)S(1)}, u32[]{:S(2)}, u32[]{:S(2)}) collective-permute-start(bf16[2,2,128,512]{3,2,1,0:T(8,128)(2,1)S(1)} %bitcast.335), channel_id=1, source_target_pairs={{0,16},{4,20},{8,24},{12,28},{16,0},{20,4},{24,8},{28,12},{1,17},{... | collective-permute-start | bytes 1572872 | tf_op jit(solution)/shard_map/ppermute | solution.py:55
  123.0 17.6 %collective-permute-start.30 = (bf16[2,2,128,512]{3,2,1,0:T(8,128)(2,1)S(1)}, bf16[2,2,128,512]{3,2,1,0:T(8,128)(2,1)S(1)}, u32[]{:S(2)}, u32[]{:S(2)}) collective-permute-start(bf16[2,2,128,512]{3,2,1,0:T(8,128)(2,1)S(1)} %bitcast.358), channel_id=1, source_target_pairs={{0,12},{4,8},{8,4},{12,0},{16,28},{20,24},{24,20},{28,16},{1,13},{... | collective-permute-start | bytes 1572872 | tf_op jit(solution)/shard_map/ppermute | solution.py:55
  123.0 17.7 %collective-permute-start.31 = (bf16[2,2,128,512]{3,2,1,0:T(8,128)(2,1)S(1)}, bf16[2,2,128,512]{3,2,1,0:T(8,128)(2,1)S(1)}, u32[]{:S(2)}, u32[]{:S(2)}) collective-permute-start(bf16[2,2,128,512]{3,2,1,0:T(8,128)(2,1)S(1)} %bitcast.359), channel_id=1, source_target_pairs={{0,4},{4,0},{8,12},{12,8},{16,20},{20,16},{24,28},{28,24},{1,5},{5... | collective-permute-start | bytes 1572872 | tf_op jit(solution)/shard_map/ppermute | solution.py:55
  131.6 9.8 %collective-permute-start.32 = (bf16[2,2,128,512]{3,2,1,0:T(8,128)(2,1)S(1)}, bf16[2,2,128,512]{3,2,1,0:T(8,128)(2,1)S(1)}, u32[]{:S(2)}, u32[]{:S(2)}) collective-permute-start(bf16[2,2,128,512]{3,2,1,0:T(8,128)(2,1)S(1)} %bitcast.332), channel_id=1, source_target_pairs={{0,16},{4,20},{8,24},{12,28},{16,0},{20,4},{24,8},{28,12},{1,17},{... | collective-permute-start | bytes 1572872 | tf_op jit(solution)/shard_map/ppermute | solution.py:55
  149.6 10.7 %collective-permute-start.34 = (bf16[2,8,32,384]{3,2,1,0:T(8,128)(2,1)S(1)}, bf16[2,8,32,384]{3,2,1,0:T(8,128)(2,1)S(1)}, u32[]{:S(2)}, u32[]{:S(2)}) collective-permute-start(bf16[2,8,32,384]{3,2,1,0:T(8,128)(2,1)S(1)} %pad_maximum_fusion.31), channel_id=1, source_target_pairs={{0,1},{1,0},{2,3},{3,2},{4,5},{5,4},{6,7},{7,6},{8,9},{9,8},{10,11... | collective-permute-start | bytes 1179656 | tf_op jit(solution)/shard_map/ppermute | solution.py:59
  149.8 11.9 %collective-permute-start.35 = (bf16[2,8,32,384]{3,2,1,0:T(8,128)(2,1)S(1)}, bf16[2,8,32,384]{3,2,1,0:T(8,128)(2,1)S(1)}, u32[]{:S(2)}, u32[]{:S(2)}) collective-permute-start(bf16[2,8,32,384]{3,2,1,0:T(8,128)(2,1)S(1)} %pad_maximum_fusion.32), channel_id=1, source_target_pairs={{0,3},{1,2},{2,1},{3,0},{4,7},{5,6},{6,5},{7,4},{8,11},{9,10},{10,... | collective-permute-start | bytes 1179656 | tf_op jit(solution)/shard_map/ppermute | solution.py:59
  (31 other events, 146.8 us)
